TPU v7x, 256 devices: a whole 4x4x8 slice. The times are simulated.
256 devices in a mesh: section: 8 (over y_lo, x), dp: 32 (over y_hi, z, core).
Axes of the slice: x: 4, y: 4 (y_hi: 2, y_lo: 2; y = y_hi * 2 + y_lo), z: 8, core: 2. Of those that a mesh axis runs over, the one named last changes fastest.
Arguments:
- saved_inputs: bfloat16 [8, 4, 2048, 1024], P('section', None, 'dp'), may hold values from -6 to 6
- norm_gain: float32 [8, 1024], P('section'), may hold values from 0.1 to 1.9
- down_weight: bfloat16 [8, 1024, 2048], P('section'), may hold values from -0.1875 to 0.1875
- up_weight: bfloat16 [8, 1024, 2048], P('section'), may hold values from -0.125 to 0.125
- head_weight: bfloat16 [1024, 128], P('dp'), may hold values from -0.1875 to 0.1875
- head_gain: float32 [1024], replicated, may hold values from 0.1 to 1.9
- targets: float32 [4, 2048, 64], P(None, 'dp'), may hold values from -6 to 6
- levels: float32 [64, 8], replicated, may hold values from -3 to 3
- level_index: int32 [64], replicated, may hold values from 0 to 7
- plan: int32 [4], replicated, may hold values from 0 to 3, each once
Outputs:
- input_grads: bfloat16 [8, 4, 2048, 1024], P('section', None, 'dp')
- down_grad: float32 [8, 1024, 2048], P('section', 'dp')
- up_grad: float32 [8, 1024, 2048], P('section', 'dp')
- head_grad: float32 [1024, 128], P(('section', 'dp'))
Inputs may be any that keep to these rules, and one draw needn't show every extreme that they name: `plan`: a permutation of the 4 micro-batches.
All inputs are finite; a program needn't handle non-finite values.
Results may differ from a plain program's by a relative error of at most 0.03.
Values may be sent and summed in bfloat16 or wider, within the bound.
A program may use at most 128 MiB of HBM per device.

v0:
```python
import functools

import jax
import jax.numpy as jnp
from jax import lax
from jax.sharding import PartitionSpec as P

VARS = 64
ENS = 2


EPS = 1e-06
DELTA = 0.25
BETA = 0.25
LOSS_SCALE = 64.0
SQRT_HALF = 0.7071067811865476
INV_SQRT_TAU = 0.3989422804014327
CONTRACT_ROWS = (((0,), (0,)), ((), ()))


def passed_along(value, axis, steps):
    count = lax.axis_size(axis)
    initial, last = (max(0, -steps), min(count, count - steps))
    return lax.ppermute(value, axis, [(source, source + steps) for source in range(initial, last)])


def norm_forward(values, scaling):
    inverse = lax.rsqrt(jnp.mean(values * values, axis=-1, keepdims=True) + EPS)
    return (values * inverse * scaling, inverse)


def norm_backward(values, inverse, scaling, upstream):
    weighted = upstream * scaling
    return inverse * weighted - values * inverse**3 * jnp.mean(
        weighted * values, axis=-1, keepdims=True
    )


def gelu_value(hidden):
    return 0.5 * hidden * (1.0 + lax.erf(hidden * SQRT_HALF))


def gelu_slope(hidden):
    return (
        0.5 * (1.0 + lax.erf(hidden * SQRT_HALF))
        + hidden * jnp.exp(-0.5 * hidden * hidden) * INV_SQRT_TAU
    )


def chained(values, threshold):
    shifted = (values - threshold) / BETA
    return (threshold + BETA * jax.nn.softplus(shifted), jax.nn.sigmoid(shifted))


def crps_slope(predicted, observed, threshold):
    columns = predicted.reshape(predicted.shape[0], ENS, VARS)
    chain_pred, chain_rate = chained(columns, threshold)
    chain_obs, unused_rate = chained(observed, threshold)
    spread_obs = chain_pred - chain_obs[:, None, :]
    term_obs = spread_obs / jnp.sqrt(spread_obs * spread_obs + DELTA * DELTA)
    pairs = chain_pred[:, :, None, :] - chain_pred[:, None, :, :]
    term_pair = jnp.sum(pairs / jnp.sqrt(pairs * pairs + DELTA * DELTA), axis=2)
    slope = chain_rate * (term_obs / ENS - term_pair / (ENS * ENS))
    return (LOSS_SCALE * slope).reshape(predicted.shape)


def section_forward(inputs, scaling, down_local, up_local):
    wide = inputs.astype(jnp.float32)
    normed_wide, inverse = norm_forward(wide, scaling)
    normed = normed_wide.astype(jnp.bfloat16)
    hidden = jnp.dot(normed, down_local, preferred_element_type=jnp.float32)
    active = gelu_value(hidden).astype(jnp.bfloat16)
    branch = lax.dot_general(
        active, up_local, (((1,), (1,)), ((), ())), preferred_element_type=jnp.float32
    )
    output = (wide + branch).astype(jnp.bfloat16)
    return (wide, inverse, normed, hidden, active, output)


def head_backward(output, full_head, head_scaling, observed, threshold):
    wide = output.astype(jnp.float32)
    normed_wide, inverse = norm_forward(wide, head_scaling)
    head_in = normed_wide.astype(jnp.bfloat16)
    predicted = jnp.dot(head_in, full_head, preferred_element_type=jnp.float32)
    head_slope = crps_slope(predicted, observed, threshold).astype(jnp.bfloat16)
    upstream = lax.dot_general(
        head_slope, full_head, (((1,), (1,)), ((), ())), preferred_element_type=jnp.float32
    )
    cotangent = norm_backward(wide, inverse, head_scaling, upstream).astype(jnp.bfloat16)
    return (cotangent, head_in, head_slope)


def section_backward(cotangent, wide, inverse, scaling, hidden, down_local, up_local):
    back_active = jnp.dot(cotangent, up_local, preferred_element_type=jnp.float32)
    back_hidden = (back_active * gelu_slope(hidden)).astype(jnp.bfloat16)
    back_normed = lax.dot_general(
        back_hidden, down_local, (((1,), (1,)), ((), ())), preferred_element_type=jnp.float32
    )
    grad_in = (
        cotangent.astype(jnp.float32) + norm_backward(wide, inverse, scaling, back_normed)
    ).astype(jnp.bfloat16)
    return (back_hidden, grad_in)


def place_slot(store, value, slot_clip, valid):
    current = lax.dynamic_index_in_dim(store, slot_clip, 0, keepdims=False)
    return lax.dynamic_update_index_in_dim(store, jnp.where(valid, value, current), slot_clip, 0)


def flatten(store):
    return store.reshape(store.shape[0] * store.shape[1], store.shape[2])


def local(
    saved_inputs,
    norm_gain,
    down_weight,
    up_weight,
    head_weight,
    head_gain,
    targets,
    levels,
    level_index,
    plan,
):
    sections = lax.axis_size("section")
    position = lax.axis_index("section")
    is_last = position == sections - 1
    micro = saved_inputs.shape[1]
    tokens_here = saved_inputs.shape[2]
    width = saved_inputs.shape[3]
    inputs_here = saved_inputs[0]
    scaling = norm_gain[0]
    down_local = down_weight[0]
    up_local = up_weight[0]
    units = down_local.shape[1]
    full_head = lax.all_gather(head_weight, "dp", axis=0, tiled=True)
    head_cols = full_head.shape[1]
    picker = lax.broadcasted_iota(jnp.int32, levels.shape, 1) == level_index[:, None]
    threshold = jnp.sum(jnp.where(picker, levels, 0.0), axis=1)

    def tick(tick_number, carried, with_head):
        (
            incoming,
            grad_store,
            cot_store,
            active_store,
            normed_store,
            hidden_store,
            head_in_store,
            head_slope_store,
        ) = carried
        slot_index = tick_number - (sections - 1 - position)
        valid = (slot_index >= 0) & (slot_index < micro)
        slot_clip = jnp.clip(slot_index, 0, micro - 1)
        batch = plan[slot_clip]
        inputs = lax.dynamic_index_in_dim(inputs_here, batch, 0, keepdims=False)
        wide, inverse, normed, hidden, active, output = section_forward(
            inputs, scaling, down_local, up_local
        )
        observed = lax.dynamic_index_in_dim(targets, batch, 0, keepdims=False)
        head_cot, head_in, head_slope = head_backward(
            output, full_head, head_gain, observed, threshold
        )
        cotangent = jnp.where(is_last, head_cot, incoming)
        head_slope = jnp.where(is_last, head_slope, jnp.zeros_like(head_slope))
        head_in_store = place_slot(head_in_store, head_in, slot_clip, valid)
        head_slope_store = place_slot(head_slope_store, head_slope, slot_clip, valid)
        back_hidden, grad_in = section_backward(
            cotangent, wide, inverse, scaling, hidden, down_local, up_local
        )
        grad_store = place_slot(grad_store, grad_in, slot_clip, valid)
        cot_store = place_slot(cot_store, cotangent, slot_clip, valid)
        active_store = place_slot(active_store, active, slot_clip, valid)
        normed_store = place_slot(normed_store, normed, slot_clip, valid)
        hidden_store = place_slot(hidden_store, back_hidden, slot_clip, valid)
        incoming = passed_along(grad_in, "section", -1)
        return (
            incoming,
            grad_store,
            cot_store,
            active_store,
            normed_store,
            hidden_store,
            head_in_store,
            head_slope_store,
        )

    wide_zero = jnp.zeros((micro, tokens_here, width), jnp.bfloat16)
    unit_zero = jnp.zeros((micro, tokens_here, units), jnp.bfloat16)
    initial = (
        jnp.zeros((tokens_here, width), jnp.bfloat16),
        wide_zero,
        wide_zero,
        unit_zero,
        wide_zero,
        unit_zero,
        wide_zero,
        jnp.zeros((micro, tokens_here, head_cols), jnp.bfloat16),
    )
    carried = lax.fori_loop(
        0, micro + sections - 1, functools.partial(tick, with_head=True), initial
    )
    head_in_all = flatten(carried[6])
    head_slope_all = flatten(carried[7])
    head_sum = lax.psum_scatter(
        lax.dot_general(
            head_in_all, head_slope_all, CONTRACT_ROWS, preferred_element_type=jnp.float32
        ),
        ("section", "dp"),
        scatter_dimension=0,
        tiled=True,
    )
    normed_all = flatten(carried[4])
    hidden_all = flatten(carried[5])
    cot_all = flatten(carried[2])
    active_all = flatten(carried[3])
    down_part = lax.dot_general(
        normed_all, hidden_all, CONTRACT_ROWS, preferred_element_type=jnp.float32
    )
    up_part = lax.dot_general(
        cot_all, active_all, CONTRACT_ROWS, preferred_element_type=jnp.float32
    )
    summed = lax.psum_scatter(
        jnp.concatenate([down_part, up_part], axis=1).astype(jnp.bfloat16),
        "dp",
        scatter_dimension=0,
        tiled=True,
    ).astype(jnp.float32)
    down_grad = (summed[:, :units] / LOSS_SCALE)[None]
    up_grad = (summed[:, units:] / LOSS_SCALE)[None]
    return (carried[1][None], down_grad, up_grad, head_sum / LOSS_SCALE)


def solution(mesh):
    placed = (
        P("section", None, "dp", None),
        P("section", None),
        P("section", None, None),
        P("section", None, None),
        P("dp", None),
        P(),
        P(None, "dp", None),
        P(),
        P(),
        P(),
    )
    return jax.shard_map(
        local,
        mesh=mesh,
        in_specs=placed,
        out_specs=(
            P("section", None, "dp", None),
            P("section", "dp", None),
            P("section", "dp", None),
            P(("section", "dp"), None),
        ),
        check_vma=False,
    )
```

profile of v0, /device:TPU:1, one launch (start us, length us, event | category | flops | bytes accessed | tf_op | source)
XLA Modules:
  0.0 660.0 jit_solution(14634902879683015942)
XLA Ops:
  8.1 47.3 %all_gather.3 = bf16[1024,128]{1,0:T(8,128)(2,1)S(1)} all-gather(bf16[32,128]{1,0:T(8,128)(2,1)} %param.16), channel_id=1, replica_groups=mesh['section'=8,'dp'=32] {'dp'}, dimensions={0}, use_global_device_ids=true | all-gather | bytes 270336 | tf_op jit(solution)/shard_map/all_gather | solution.py:137
  60.1 315.5 %while.29 = (s32[]{:T(128)}, bf16[64,1024]{1,0:T(8,128)(2,1)S(1)}, bf16[4,64,1024]{2,1,0:T(8,128)(2,1)}, bf16[4,64,1024]{2,1,0:T(8,128)(2,1)}, bf16[4,64,2048]{2...) while((s32[]{:T(128)}, bf16[64,1024]{1,0:T(8,128)(2,1)S(1)}, ...), condition=%wide.region_7.8_spmd, body=%wide.region_1.7_spmd.sunk | while | flops 1113661696 | bytes 70014480 | solution.py:201
  65.8 4.0 bitcast_dynamic-update-slice_fusion.11
  74.3 3.9 bitcast_dynamic-update-slice_fusion.14
  82.8 5.5 collective-permute-done
  94.0 4.0 bitcast_dynamic-update-slice_fusion.11
  102.6 3.9 bitcast_dynamic-update-slice_fusion.14
  111.0 4.4 collective-permute-done
  121.1 4.0 bitcast_dynamic-update-slice_fusion.11
  138.1 4.4 collective-permute-done
  148.3 4.0 bitcast_dynamic-update-slice_fusion.11
  165.2 6.0 collective-permute-done
  177.0 4.0 bitcast_dynamic-update-slice_fusion.11
  194.0 6.0 collective-permute-done
  205.7 4.0 bitcast_dynamic-update-slice_fusion.11
  222.7 6.5 collective-permute-done
  234.9 4.0 bitcast_dynamic-update-slice_fusion.11
  251.9 6.5 collective-permute-done
  264.1 4.0 bitcast_dynamic-update-slice_fusion.11
  281.1 6.6 %collective-permute-done = bf16[64,1024]{1,0:T(8,128)(2,1)S(1)} collective-permute-done((bf16[64,1024]{1,0:T(8,128)(2,1)S(1)}, bf16[64,1024]{1,0:T(8,128)(2,1)S(1)}, u32[]{:S(2)}, u32[]{:S(2)}) %collective-permute-start) | collective-permute-done | bytes 131104 | tf_op jit(solution)/shard_map/while/body/eval_jaxpr/ppermute | solution.py:24
  293.5 4.0 bitcast_dynamic-update-slice_fusion.11
  302.0 3.9 bitcast_dynamic-update-slice_fusion.14
  310.5 6.4 collective-permute-done
  322.6 4.0 bitcast_dynamic-update-slice_fusion.11
  331.1 3.9 bitcast_dynamic-update-slice_fusion.14
  339.6 6.6 %collective-permute-done = bf16[64,1024]{1,0:T(8,128)(2,1)S(1)} collective-permute-done((bf16[64,1024]{1,0:T(8,128)(2,1)S(1)}, bf16[64,1024]{1,0:T(8,128)(2,1)S(1)}, u32[]{:S(2)}, u32[]{:S(2)}) %collective-permute-start) | collective-permute-done | bytes 131104 | tf_op jit(solution)/shard_map/while/body/eval_jaxpr/ppermute | solution.py:24
  352.0 4.0 bitcast_dynamic-update-slice_fusion.11
  360.5 3.9 bitcast_dynamic-update-slice_fusion.14
  369.0 6.5 collective-permute-done
  376.8 4.7 bitcast_convert_fusion
  384.7 7.8 %pad_maximum_fusion = bf16[1024,4096]{1,0:T(8,128)(2,1)} fusion(bf16[1024,2048]{1,0:T(8,128)(2,1)} %bitcast_convert_fusion, bf16[1024,2048]{1,0:T(8,128)(2,1)} %bitcast_convert_fusion.1), kind=kLoop, calls=%fused_computation.88 | loop fusion | flops 16777216 | bytes 16777216 | tf_op jit(solution)/shard_map/concatenate | solution.py:225
  392.5 257.0 %all-reduce.3.cloned.1.call-done = f32[1024,128]{1,0:T(8,128)} async-done(((f32[1024,128]{1,0:T(8,128)}), f32[1024,128]{1,0:T(8,128)}) %all-reduce.3.cloned.1.call-update) | async-done | bytes 524304
  (453 shorter events, 176.4 us)
Async XLA Ops:
  8.0 52.1 %copy-start.8 = (s32[4]{0:T(128)S(1)}, s32[4]{0:T(128)}, u32[]{:S(2)}) copy-start(s32[4]{0:T(128)} %param.21) | copy-start | bytes 52
  8.0 52.0 %copy-start.6 = (f32[1024]{0:T(1024)S(1)}, f32[1024]{0:T(1024)}, u32[]{:S(2)}) copy-start(f32[1024]{0:T(1024)} %param.17) | copy-start | bytes 12292
  8.0 52.0 %copy-start.7 = (f32[1,1024]{1,0:T(1,128)S(1)}, f32[1,1024]{1,0:T(1,128)}, u32[]{:S(2)}) copy-start(f32[1,1024]{1,0:T(1,128)} %param.13) | copy-start | bytes 12292
  8.0 52.0 %copy-start.2 = (bf16[1,4,64,1024]{3,2,1,0:T(8,128)(2,1)S(1)}, bf16[1,4,64,1024]{3,2,1,0:T(8,128)(2,1)}, u32[]{:S(2)}) copy-start(bf16[1,4,64,1024]{3,2,1,0:T(8,128)(2,1)} %param.12) | copy-start | bytes 1572868
  8.0 641.4 %all-reduce.3.cloned.1.call-start = ((), (), s32[]{:S(2)}) async-start(), calls=%async_computation.2 | async-start | bytes 1048576
  78.2 10.1 %copy-start.4 = (bf16[4,64,2048]{2,1,0:T(8,128)(2,1)S(1)}, bf16[4,64,2048]{2,1,0:T(8,128)(2,1)}, u32[]{:S(2)}) copy-start(bf16[4,64,2048]{2,1,0:T(8,128)(2,1)} %get-tuple-element.746) | copy-start | bytes 3145732 | tf_op jit(solution)/shard_map/while
  81.5 6.8 %collective-permute-start = (bf16[64,1024]{1,0:T(8,128)(2,1)S(1)}, bf16[64,1024]{1,0:T(8,128)(2,1)S(1)}, u32[]{:S(2)}, u32[]{:S(2)}) collective-permute-start(bf16[64,1024]{1,0:T(8,128)(2,1)S(1)} %get-tuple-element.684), channel_id=1, source_target_pairs={{32,0},{64,32},{96,64},{128,96},{160,128},{192,160},{224,192},{33,... | collective-permute-start | bytes 393224 | tf_op jit(solution)/shard_map/while/body/eval_jaxpr/ppermute | solution.py:24
  100.2 6.3 copy-start
  106.4 9.0 %copy-start.4 = (bf16[4,64,2048]{2,1,0:T(8,128)(2,1)S(1)}, bf16[4,64,2048]{2,1,0:T(8,128)(2,1)}, u32[]{:S(2)}) copy-start(bf16[4,64,2048]{2,1,0:T(8,128)(2,1)} %get-tuple-element.746) | copy-start | bytes 3145732 | tf_op jit(solution)/shard_map/while
  109.7 5.7 collective-permute-start
  133.6 9.0 %copy-start.4 = (bf16[4,64,2048]{2,1,0:T(8,128)(2,1)S(1)}, bf16[4,64,2048]{2,1,0:T(8,128)(2,1)}, u32[]{:S(2)}) copy-start(bf16[4,64,2048]{2,1,0:T(8,128)(2,1)} %get-tuple-element.746) | copy-start | bytes 3145732 | tf_op jit(solution)/shard_map/while
  136.8 5.7 collective-permute-start
  160.7 10.6 %copy-start.4 = (bf16[4,64,2048]{2,1,0:T(8,128)(2,1)S(1)}, bf16[4,64,2048]{2,1,0:T(8,128)(2,1)}, u32[]{:S(2)}) copy-start(bf16[4,64,2048]{2,1,0:T(8,128)(2,1)} %get-tuple-element.746) | copy-start | bytes 3145732 | tf_op jit(solution)/shard_map/while
  163.9 7.3 %collective-permute-start = (bf16[64,1024]{1,0:T(8,128)(2,1)S(1)}, bf16[64,1024]{1,0:T(8,128)(2,1)S(1)}, u32[]{:S(2)}, u32[]{:S(2)}) collective-permute-start(bf16[64,1024]{1,0:T(8,128)(2,1)S(1)} %get-tuple-element.684), channel_id=1, source_target_pairs={{32,0},{64,32},{96,64},{128,96},{160,128},{192,160},{224,192},{33,... | collective-permute-start | bytes 393224 | tf_op jit(solution)/shard_map/while/body/eval_jaxpr/ppermute | solution.py:24
  189.4 10.6 %copy-start.4 = (bf16[4,64,2048]{2,1,0:T(8,128)(2,1)S(1)}, bf16[4,64,2048]{2,1,0:T(8,128)(2,1)}, u32[]{:S(2)}) copy-start(bf16[4,64,2048]{2,1,0:T(8,128)(2,1)} %get-tuple-element.746) | copy-start | bytes 3145732 | tf_op jit(solution)/shard_map/while
  192.7 7.3 %collective-permute-start = (bf16[64,1024]{1,0:T(8,128)(2,1)S(1)}, bf16[64,1024]{1,0:T(8,128)(2,1)S(1)}, u32[]{:S(2)}, u32[]{:S(2)}) collective-permute-start(bf16[64,1024]{1,0:T(8,128)(2,1)S(1)} %get-tuple-element.684), channel_id=1, source_target_pairs={{32,0},{64,32},{96,64},{128,96},{160,128},{192,160},{224,192},{33,... | collective-permute-start | bytes 393224 | tf_op jit(solution)/shard_map/while/body/eval_jaxpr/ppermute | solution.py:24
  218.1 11.1 %copy-start.4 = (bf16[4,64,2048]{2,1,0:T(8,128)(2,1)S(1)}, bf16[4,64,2048]{2,1,0:T(8,128)(2,1)}, u32[]{:S(2)}) copy-start(bf16[4,64,2048]{2,1,0:T(8,128)(2,1)} %get-tuple-element.746) | copy-start | bytes 3145732 | tf_op jit(solution)/shard_map/while
  221.4 7.8 %collective-permute-start = (bf16[64,1024]{1,0:T(8,128)(2,1)S(1)}, bf16[64,1024]{1,0:T(8,128)(2,1)S(1)}, u32[]{:S(2)}, u32[]{:S(2)}) collective-permute-start(bf16[64,1024]{1,0:T(8,128)(2,1)S(1)} %get-tuple-element.684), channel_id=1, source_target_pairs={{32,0},{64,32},{96,64},{128,96},{160,128},{192,160},{224,192},{33,... | collective-permute-start | bytes 393224 | tf_op jit(solution)/shard_map/while/body/eval_jaxpr/ppermute | solution.py:24
  247.3 11.1 %copy-start.4 = (bf16[4,64,2048]{2,1,0:T(8,128)(2,1)S(1)}, bf16[4,64,2048]{2,1,0:T(8,128)(2,1)}, u32[]{:S(2)}) copy-start(bf16[4,64,2048]{2,1,0:T(8,128)(2,1)} %get-tuple-element.746) | copy-start | bytes 3145732 | tf_op jit(solution)/shard_map/while
  250.6 7.8 %collective-permute-start = (bf16[64,1024]{1,0:T(8,128)(2,1)S(1)}, bf16[64,1024]{1,0:T(8,128)(2,1)S(1)}, u32[]{:S(2)}, u32[]{:S(2)}) collective-permute-start(bf16[64,1024]{1,0:T(8,128)(2,1)S(1)} %get-tuple-element.684), channel_id=1, source_target_pairs={{32,0},{64,32},{96,64},{128,96},{160,128},{192,160},{224,192},{33,... | collective-permute-start | bytes 393224 | tf_op jit(solution)/shard_map/while/body/eval_jaxpr/ppermute | solution.py:24
  276.5 11.2 %copy-start.4 = (bf16[4,64,2048]{2,1,0:T(8,128)(2,1)S(1)}, bf16[4,64,2048]{2,1,0:T(8,128)(2,1)}, u32[]{:S(2)}) copy-start(bf16[4,64,2048]{2,1,0:T(8,128)(2,1)} %get-tuple-element.746) | copy-start | bytes 3145732 | tf_op jit(solution)/shard_map/while
  279.8 7.9 %collective-permute-start = (bf16[64,1024]{1,0:T(8,128)(2,1)S(1)}, bf16[64,1024]{1,0:T(8,128)(2,1)S(1)}, u32[]{:S(2)}, u32[]{:S(2)}) collective-permute-start(bf16[64,1024]{1,0:T(8,128)(2,1)S(1)} %get-tuple-element.684), channel_id=1, source_target_pairs={{32,0},{64,32},{96,64},{128,96},{160,128},{192,160},{224,192},{33,... | collective-permute-start | bytes 393224 | tf_op jit(solution)/shard_map/while/body/eval_jaxpr/ppermute | solution.py:24
  299.6 6.3 copy-start
  305.9 11.0 %copy-start.4 = (bf16[4,64,2048]{2,1,0:T(8,128)(2,1)S(1)}, bf16[4,64,2048]{2,1,0:T(8,128)(2,1)}, u32[]{:S(2)}) copy-start(bf16[4,64,2048]{2,1,0:T(8,128)(2,1)} %get-tuple-element.746) | copy-start | bytes 3145732 | tf_op jit(solution)/shard_map/while
  309.2 7.7 %collective-permute-start = (bf16[64,1024]{1,0:T(8,128)(2,1)S(1)}, bf16[64,1024]{1,0:T(8,128)(2,1)S(1)}, u32[]{:S(2)}, u32[]{:S(2)}) collective-permute-start(bf16[64,1024]{1,0:T(8,128)(2,1)S(1)} %get-tuple-element.684), channel_id=1, source_target_pairs={{32,0},{64,32},{96,64},{128,96},{160,128},{192,160},{224,192},{33,... | collective-permute-start | bytes 393224 | tf_op jit(solution)/shard_map/while/body/eval_jaxpr/ppermute | solution.py:24
  328.8 6.3 copy-start
  335.0 11.2 %copy-start.4 = (bf16[4,64,2048]{2,1,0:T(8,128)(2,1)S(1)}, bf16[4,64,2048]{2,1,0:T(8,128)(2,1)}, u32[]{:S(2)}) copy-start(bf16[4,64,2048]{2,1,0:T(8,128)(2,1)} %get-tuple-element.746) | copy-start | bytes 3145732 | tf_op jit(solution)/shard_map/while
  338.3 7.9 %collective-permute-start = (bf16[64,1024]{1,0:T(8,128)(2,1)S(1)}, bf16[64,1024]{1,0:T(8,128)(2,1)S(1)}, u32[]{:S(2)}, u32[]{:S(2)}) collective-permute-start(bf16[64,1024]{1,0:T(8,128)(2,1)S(1)} %get-tuple-element.684), channel_id=1, source_target_pairs={{32,0},{64,32},{96,64},{128,96},{160,128},{192,160},{224,192},{33,... | collective-permute-start | bytes 393224 | tf_op jit(solution)/shard_map/while/body/eval_jaxpr/ppermute | solution.py:24
  358.1 6.3 copy-start
  364.4 11.1 %copy-start.4 = (bf16[4,64,2048]{2,1,0:T(8,128)(2,1)S(1)}, bf16[4,64,2048]{2,1,0:T(8,128)(2,1)}, u32[]{:S(2)}) copy-start(bf16[4,64,2048]{2,1,0:T(8,128)(2,1)} %get-tuple-element.746) | copy-start | bytes 3145732 | tf_op jit(solution)/shard_map/while
  367.7 7.8 %collective-permute-start = (bf16[64,1024]{1,0:T(8,128)(2,1)S(1)}, bf16[64,1024]{1,0:T(8,128)(2,1)S(1)}, u32[]{:S(2)}, u32[]{:S(2)}) collective-permute-start(bf16[64,1024]{1,0:T(8,128)(2,1)S(1)} %get-tuple-element.684), channel_id=1, source_target_pairs={{32,0},{64,32},{96,64},{128,96},{160,128},{192,160},{224,192},{33,... | collective-permute-start | bytes 393224 | tf_op jit(solution)/shard_map/while/body/eval_jaxpr/ppermute | solution.py:24
  376.7 274.0 %reduce-scatter.2.cloned.1.call-start = ((), (), s32[]{:S(2)}) async-start(), calls=%async_computation.1 | async-start | bytes 8650752 | tf_op jit(solution)/shard_map/reduce_scatter | solution.py:224
  (30 other events, 144.5 us)
Sparse Core Ops, SparseCore 0:
  376.8 272.6 all-reduce.2
Sparse Core Ops, SparseCore 1:
  392.6 162.6 reduce-scatter.1
where the time goes:
time: 663 us; the launch traced here: 660 us
  waiting for transfers between devices  323 us (49%)
  matrix products  135 us (20%)
  other arithmetic  65.3 us (10%)
  blocking collectives  47.3 us (7%)
  local copies, waits for them, and re-layouts  38.1 us (6%)
  loops' own time  22.1 us (3%)
  between operations  15.6 us (2%)
  starting transfers between devices  14.2 us (2%)
    unnamed x3, waiting for transfers between devices  257 us
    ppermute x11, waiting for transfers between devices, passed_along(): lax.ppermute(value, axis, [(source, source + steps) for source in range(i...  65.6 us
    all_gather x1, blocking collectives, local(): full_head = lax.all_gather(head_weight, 'dp', axis=0, tiled=True)  47.3 us
    dot_general x11, matrix products, section_forward(): hidden = jnp.dot(normed, down_local, preferred_element_type=jnp.float32)  44.1 us
    dot_general x11, matrix products, section_backward(): jnp.dot(cotangent, up_local, preferred_element_type=jnp.float32)  42.8 us
    dynamic_update_slice x33, other arithmetic, place_slot(): lax.dynamic_update_index_in_dim(store, jnp.where(valid, value, current),...  42.2 us
    another operation x1, loops' own time, local(): lax.fori_loop(0, micro + sections - 1, functools.partial(tick, with_head=...  22.1 us
    dynamic_slice x55, local copies, waits for them, and re-layouts, place_slot(): current = lax.dynamic_index_in_dim(store, slot_clip, 0, keepdims=False)  21.3 us
  transfers between devices with their start and end apart: 13, of which 12 were waited for; matrix products, arithmetic and copies ran while one was open for 3% of the time, Pallas kernels for 0%

commit v1 on v0

v1 whole, which is shorter than its diff:
```python
import functools

import jax
import jax.numpy as jnp
from jax import lax
from jax.experimental import pallas as pl
from jax.experimental.pallas import tpu as pltpu
from jax.sharding import PartitionSpec as P

EPS = 1e-06
DELTA = 0.25
BETA = 0.25
LOSS_SCALE = 64.0
SQRT_HALF = 0.7071067811865476
INV_SQRT_TAU = 0.3989422804014327
MESH = pl.DeviceIdType.MESH
F32 = jnp.float32
BF16 = jnp.bfloat16
NN = (((1,), (0,)), ((), ()))
NT = (((1,), (1,)), ((), ()))
TN = (((0,), (0,)), ((), ()))


def matmul(left, right, dims=NN):
    return lax.dot_general(left, right, dims, preferred_element_type=F32)


def inverse_rms(values):
    return lax.rsqrt(jnp.mean(values * values, axis=-1, keepdims=True) + EPS)


def norm_backward(values, inverse, scaling, upstream):
    weighted = upstream * scaling
    mean = jnp.mean(weighted * values, axis=-1, keepdims=True)
    return inverse * weighted - values * (inverse * inverse * inverse) * mean


def soft(values):
    return values * lax.rsqrt(values * values + DELTA * DELTA)


def chain(values, threshold):
    shifted = (values - threshold) / BETA
    softplus = jnp.maximum(shifted, 0.0) + jnp.log1p(jnp.exp(-jnp.abs(shifted)))
    return threshold + BETA * softplus


def chain_rate(values, threshold):
    shifted = (values - threshold) / BETA
    small = jnp.exp(-jnp.abs(shifted))
    return jnp.where(shifted >= 0.0, 1.0, small) / (1.0 + small)


def crps_slope(predicted, observed, threshold):
    variables = observed.shape[1]
    first, second = predicted[:, :variables], predicted[:, variables:]
    chain_first, chain_second = chain(first, threshold), chain(second, threshold)
    chain_obs = chain(observed, threshold)
    pair = soft(chain_first - chain_second)
    slope_first = soft(chain_first - chain_obs) / 2 - pair / 4
    slope_second = soft(chain_second - chain_obs) / 2 + pair / 4
    return jnp.concatenate(
        [
            LOSS_SCALE * chain_rate(first, threshold) * slope_first,
            LOSS_SCALE * chain_rate(second, threshold) * slope_second,
        ],
        axis=1,
    )


def body(
    sections,
    replicas,
    plan_ref,
    index_ref,
    saved_ref,
    gain_ref,
    down_ref,
    up_ref,
    head_ref,
    head_gain_ref,
    targets_ref,
    levels_ref,
    grads_out,
    down_out,
    up_out,
    head_out,
    saved,
    down,
    up,
    wide,
    inverses,
    normed,
    active,
    slopes,
    cots,
    backs,
    products,
    ring,
    across,
    halves,
    mates,
    full_head,
    outputs,
    head_ins,
    head_slopes,
    head_parts,
    head_terms,
    head_sums,
    head_mine,
    load_sem,
    cot_send,
    cot_recv,
    pair_send,
    pair_recv,
    slot_send,
    slot_recv,
    ring_send,
    ring_recv,
    across_send,
    across_recv,
    mate_send,
    mate_recv,
    gather_send,
    gather_recv,
    term_send,
    term_recv,
    share_send,
    share_recv,
):
    micro, tokens, width = wide.shape
    rows_all = micro * tokens
    half = active.shape[-1]
    levels = replicas // 4
    chunk = width // (2 * levels)
    share = width // replicas
    final = head_mine.shape[0]

    section = lax.axis_index("section")
    me = lax.axis_index("dp")
    core = lax.rem(me, 2)
    level = lax.rem(lax.div(me, 2), levels)
    side = lax.div(me, 2 * levels)
    is_last = section == sections - 1
    not_last = section < sections - 1
    not_first = section > 0

    def member(side_of, level_of, core_of):
        return (section, (side_of * levels + level_of) * 2 + core_of)

    ahead = member(side, lax.rem(level + 1, levels), core)
    behind = member(side, lax.rem(level + levels - 1, levels), core)
    mate = member(side, level, 1 - core)
    opposite = member(1 - side, level, core)
    sender = (lax.rem(section + 1, sections), me)
    receiver = (lax.rem(section + sections - 1, sections), me)
    head_source = lax.div(section * replicas + me, sections)
    source_is_me = jnp.logical_and(is_last, head_source == me)

    def remote(src, dst, send, recv, device):
        return pltpu.make_async_remote_copy(
            src_ref=src,
            dst_ref=dst,
            send_sem=send,
            recv_sem=recv,
            device_id=device,
            device_id_type=MESH,
        )

    saved_load = pltpu.make_async_copy(saved_ref, saved, load_sem.at[0])
    down_load = pltpu.make_async_copy(down_ref, down, load_sem.at[1])
    up_load = pltpu.make_async_copy(up_ref, up, load_sem.at[2])
    saved_load.start()
    down_load.start()
    up_load.start()

    barrier = pltpu.get_barrier_semaphore()

    def greet(device):
        pl.semaphore_signal(barrier, inc=1, device_id=device, device_id_type=MESH)

    @pl.when(not_last)
    def _():
        greet(sender)
        for device in (ahead, behind, mate, opposite):
            greet(device)

    @pl.when(is_last)
    def _():
        def greet_peer(offset, unused):
            greet((section, lax.rem(me + offset, replicas)))
            return unused

        lax.fori_loop(1, replicas, greet_peer, 0)

    @pl.when(jnp.logical_not(source_is_me))
    def _():
        greet((sections - 1, head_source))

    saved_load.wait()

    def norm_slot(slot, unused):
        values = saved[plan_ref[slot]]
        wide[slot] = values
        values = values.astype(F32)
        inverse = inverse_rms(values)
        inverses[slot] = inverse
        normed[0, slot] = (values * inverse * gain_ref[...]).astype(BF16)
        return unused

    lax.fori_loop(0, micro, norm_slot, 0)

    heard = jnp.where(
        is_last,
        replicas + sections - jnp.where(me == replicas - 1, 1, 0),
        4 + jnp.where(not_first, 1, 0),
    )
    pl.semaphore_wait(barrier, heard)

    def gather_copy(offset):
        peer = lax.rem(me + offset, replicas)
        return remote(
            head_ref, full_head.at[me], gather_send.at[offset], gather_recv.at[me], (section, peer)
        )

    def gather_wait(offset):
        peer = lax.rem(me + offset, replicas)
        remote(
            head_ref, full_head.at[peer], gather_send.at[offset], gather_recv.at[peer], (section, peer)
        ).wait_recv()

    @pl.when(is_last)
    def _():
        def send(offset, unused):
            gather_copy(offset).start()
            return unused

        lax.fori_loop(1, replicas, send, 0)
        full_head[me] = head_ref[...]

    normed_copy = remote(normed.at[0], normed.at[1], pair_send.at[0], pair_recv.at[0], mate)
    normed_copy.start()

    down_load.wait()
    step = min(256, half)
    all_normed = normed[0].reshape(rows_all, width)
    for part in range(2):
        where = 2 * lax.rem(core + part, 2)

        def forward(number, unused, part=part, where=where):
            columns = pl.ds(pl.multiple_of(part * half + number * step, step), step)
            inner = pl.ds(pl.multiple_of(number * step, step), step)
            hidden = matmul(all_normed, down[:, columns])
            bell = 0.5 * (1.0 + lax.erf(hidden * SQRT_HALF))
            active[where, :, :, inner] = (
                (hidden * bell).astype(BF16).reshape(micro, tokens, step)
            )
            slope = bell + hidden * jnp.exp(-0.5 * hidden * hidden) * INV_SQRT_TAU
            slopes[part, :, :, inner] = slope.reshape(micro, tokens, step)
            return unused

        lax.fori_loop(0, half // step, forward, 0)

    active_copy = remote(active.at[2], active.at[1], pair_send.at[1], pair_recv.at[1], mate)
    active_copy.start()
    up_load.wait()

    @pl.when(is_last)
    def _():
        wide_step = min(256, width)

        def output_columns(number, unused):
            columns = pl.ds(pl.multiple_of(number * wide_step, wide_step), wide_step)
            total = wide[:, :, columns].astype(F32).reshape(rows_all, wide_step)
            for part in range(2):
                where = 2 * lax.rem(core + part, 2)
                total = total + matmul(
                    active[where].reshape(rows_all, half),
                    up[columns, part * half : (part + 1) * half],
                    NT,
                )
            outputs[:, :, columns] = total.astype(BF16).reshape(micro, tokens, wide_step)
            return unused

        lax.fori_loop(0, width // wide_step, output_columns, 0)

        def arrive(offset, unused):
            gather_wait(offset)
            return unused

        lax.fori_loop(1, replicas, arrive, 0)

    def head_slot(slot):
        variables, count = levels_ref.shape
        diagonal = lax.broadcasted_iota(jnp.int32, (variables, variables), 0) == (
            lax.broadcasted_iota(jnp.int32, (variables, variables), 1)
        )
        threshold = jnp.zeros((1, variables), F32)
        for number in range(count):
            row = jnp.sum(
                jnp.where(diagonal, levels_ref[:, number : number + 1], 0.0), axis=0, keepdims=True
            )
            threshold = jnp.where(index_ref[...] == number, row, threshold)
        head = full_head[...].reshape(width, full_head.shape[2])
        values = outputs[slot].astype(F32)
        inverse = inverse_rms(values)
        head_in = (values * inverse * head_gain_ref[...]).astype(BF16)
        head_ins[slot] = head_in
        predicted = matmul(head_in, head)
        slope = crps_slope(predicted, targets_ref[plan_ref[slot]], threshold).astype(BF16)
        head_slopes[slot] = slope
        upstream = matmul(slope, head, NT)
        cots[0, slot] = norm_backward(values, inverse, head_gain_ref[...], upstream).astype(BF16)

    def cot_copy(slot):
        return remote(
            grads_out.at[slot], cots.at[0, slot], cot_send.at[slot], cot_recv.at[slot], receiver
        )

    def pass_cot(slot):
        return remote(
            cots.at[0, slot], cots.at[1, slot], slot_send.at[0, slot], slot_recv.at[0, slot], mate
        )

    def pass_back(slot):
        return remote(
            backs.at[2, slot], backs.at[1, slot], slot_send.at[1, slot], slot_recv.at[1, slot], mate
        )

    def backward(slot, unused):
        @pl.when(not_last)
        def _():
            cot_copy(slot).wait_recv()

        @pl.when(is_last)
        def _():
            head_slot(slot)

        pass_cot(slot).start()
        cotangent = cots[0, slot]
        back_normed = jnp.zeros((tokens, width), F32)
        for part in range(2):
            columns = slice(part * half, (part + 1) * half)
            back = (matmul(cotangent, up[:, columns]) * slopes[part, slot]).astype(BF16)
            backs[2 * lax.rem(core + part, 2), slot] = back
            back_normed = back_normed + matmul(back, down[:, columns], NT)
        grads_out[slot] = (
            cotangent.astype(F32)
            + norm_backward(wide[slot].astype(F32), inverses[slot], gain_ref[...], back_normed)
        ).astype(BF16)

        @pl.when(not_first)
        def _():
            cot_copy(slot).start()

        pass_back(slot).start()
        return unused

    lax.fori_loop(0, micro, backward, 0)

    def slot_arrived(slot, unused):
        pass_cot(slot).wait_recv()
        pass_back(slot).wait_recv()
        return unused

    normed_copy.wait_recv()
    active_copy.wait_recv()
    lax.fori_loop(0, micro, slot_arrived, 0)
    row_step = min(256, width)

    def multiply(number, unused):
        rows = pl.ds(pl.multiple_of(number * row_step, row_step), row_step)
        for matrix, left, right in ((1, cots, active), (0, normed, backs)):
            products[matrix, rows] = matmul(
                left[:, :, :, rows].reshape(2 * rows_all, row_step),
                right[0:2].reshape(2 * rows_all, half),
                TN,
            ).astype(BF16)
        return unused

    lax.fori_loop(0, width // row_step, multiply, 0)

    def term_copy(offset):
        peer = lax.rem(me + offset, replicas)
        return remote(
            head_parts.at[peer], head_terms.at[me], term_send.at[offset], term_recv.at[me], (section, peer)
        )

    def term_wait(offset):
        peer = lax.rem(me + offset, replicas)
        remote(
            head_parts.at[peer], head_terms.at[peer], term_send.at[offset], term_recv.at[peer], (section, peer)
        ).wait_recv()

    def share_copy(number):
        block = sections * me + number
        target = (lax.div(block, replicas), lax.rem(block, replicas))
        return block, remote(head_sums.at[number], head_mine, share_send.at[number], share_recv, target)

    @pl.when(is_last)
    def _():
        part = matmul(
            head_ins[...].reshape(rows_all, width),
            head_slopes[...].reshape(rows_all, head_slopes.shape[2]),
            TN,
        )
        head_parts[...] = part.reshape(head_parts.shape)

        def send(offset, unused):
            term_copy(offset).start()
            return unused

        lax.fori_loop(1, replicas, send, 0)

    def place(matrix, turn):
        if matrix == 0:
            return lax.rem(level + 2 * levels - 1 - turn, levels)
        return lax.rem(level + 1 + turn, levels)

    def rows_of(which, position):
        side_of = 1 - side if which == 0 else side
        return pl.ds(pl.multiple_of((side_of * levels + position) * chunk, chunk), chunk)

    def ring_copy(matrix, which, turn):
        return remote(
            products.at[matrix, rows_of(which, place(matrix, turn))],
            ring.at[matrix, which, turn],
            ring_send.at[matrix, which, turn],
            ring_recv.at[matrix, which, turn],
            ahead if matrix == 0 else behind,
        )

    def add_arrived(matrix, which, turn):
        ring_copy(matrix, which, turn - 1).wait_recv()
        rows = rows_of(which, place(matrix, turn))
        return products[matrix, rows].astype(F32) + ring[matrix, which, turn - 1].astype(F32)

    for which in range(2):
        for matrix in range(2):
            ring_copy(matrix, which, 0).start()

    def turn_ring(turn, unused):
        for which in range(2):
            for matrix in range(2):
                rows = rows_of(which, place(matrix, turn))
                products[matrix, rows] = add_arrived(matrix, which, turn).astype(BF16)
                ring_copy(matrix, which, turn).start()
        return unused

    lax.fori_loop(1, levels - 1, turn_ring, 0)

    def across_copy(matrix):
        return remote(
            products.at[matrix, rows_of(0, level)],
            across.at[matrix],
            across_send.at[matrix],
            across_recv.at[matrix],
            opposite,
        )

    for matrix in range(2):
        products[matrix, rows_of(0, level)] = add_arrived(matrix, 0, levels - 1).astype(BF16)
        across_copy(matrix).start()

    def mate_copy(matrix):
        return remote(
            halves.at[matrix, 1 - core], mates.at[matrix], mate_send.at[matrix], mate_recv.at[matrix], mate
        )

    mine = pl.ds(pl.multiple_of(core * half, half), half)
    theirs = pl.ds(pl.multiple_of((1 - core) * half, half), half)
    for matrix, result in ((0, down_out), (1, up_out)):
        total = add_arrived(matrix, 1, levels - 1)
        across_copy(matrix).wait_recv()
        total = (total + across[matrix].astype(F32)) / LOSS_SCALE
        halves[matrix] = total.reshape(2, share, half)
        mate_copy(matrix).start()
        result[:, mine] = halves[matrix, core]

    @pl.when(is_last)
    def _():
        def add_term(offset, total):
            term_wait(offset)
            return total + head_terms[lax.rem(me + offset, replicas)]

        total = lax.fori_loop(1, replicas, add_term, head_parts[me]) / LOSS_SCALE
        for number in range(sections):
            head_sums[number] = total[number * final : (number + 1) * final]
        for number in range(sections):
            block, copy = share_copy(number)
            to_me = block == (sections - 1) * replicas + me

            @pl.when(to_me)
            def _():
                head_mine[...] = head_sums[number]

            @pl.when(jnp.logical_not(to_me))
            def _():
                copy.start()

    for matrix, result in ((0, down_out), (1, up_out)):
        mate_copy(matrix).wait_recv()
        result[:, theirs] = mates[matrix]

    @pl.when(jnp.logical_not(source_is_me))
    def _():
        share_copy(0)[1].wait_recv()

    head_out[...] = head_mine[...]

    normed_copy.wait_send()
    active_copy.wait_send()

    def slot_left(slot, unused):
        pass_cot(slot).wait_send()
        pass_back(slot).wait_send()
        return unused

    lax.fori_loop(0, micro, slot_left, 0)

    @pl.when(not_first)
    def _():
        def cot_left(slot, unused):
            cot_copy(slot).wait_send()
            return unused

        lax.fori_loop(0, micro, cot_left, 0)

    def ring_left(turn, unused):
        for which in range(2):
            for matrix in range(2):
                ring_copy(matrix, which, turn).wait_send()
        return unused

    lax.fori_loop(0, levels - 1, ring_left, 0)
    for matrix in range(2):
        across_copy(matrix).wait_send()
        mate_copy(matrix).wait_send()

    @pl.when(is_last)
    def _():
        def head_left(offset, unused):
            gather_copy(offset).wait_send()
            term_copy(offset).wait_send()
            return unused

        lax.fori_loop(1, replicas, head_left, 0)
        for number in range(sections):
            block, copy = share_copy(number)

            @pl.when(block != (sections - 1) * replicas + me)
            def _():
                copy.wait_send()


def local(
    sections,
    replicas,
    saved_inputs,
    norm_gain,
    down_weight,
    up_weight,
    head_weight,
    head_gain,
    targets,
    levels,
    level_index,
    plan,
):
    micro, tokens, width = saved_inputs.shape[1:]
    units = down_weight.shape[2]
    half = units // 2
    cols = head_weight.shape[1]
    rings = replicas // 4
    chunk = width // (2 * rings)
    share = width // replicas
    final = share // sections
    whole = pl.BlockSpec(memory_space=pltpu.VMEM)
    anywhere = pl.BlockSpec(memory_space=pl.ANY)
    dma = pltpu.SemaphoreType.DMA
    grads, down_grad, up_grad, head_grad = pl.pallas_call(
        functools.partial(body, sections, replicas),
        out_shape=(
            jax.ShapeDtypeStruct((micro, tokens, width), BF16),
            jax.ShapeDtypeStruct((share, units), F32),
            jax.ShapeDtypeStruct((share, units), F32),
            jax.ShapeDtypeStruct((final, cols), F32),
        ),
        in_specs=[
            pl.BlockSpec(memory_space=pltpu.SMEM),
            whole,
            anywhere,
            whole,
            anywhere,
            anywhere,
            whole,
            whole,
            whole,
            whole,
        ],
        out_specs=(whole, whole, whole, whole),
        scratch_shapes=[
            pltpu.VMEM((micro, tokens, width), BF16),
            pltpu.VMEM((width, units), BF16),
            pltpu.VMEM((width, units), BF16),
            pltpu.VMEM((micro, tokens, width), BF16),
            pltpu.VMEM((micro, tokens, 1), F32),
            pltpu.VMEM((2, micro, tokens, width), BF16),
            pltpu.VMEM((3, micro, tokens, half), BF16),
            pltpu.VMEM((2, micro, tokens, half), F32),
            pltpu.VMEM((2, micro, tokens, width), BF16),
            pltpu.VMEM((3, micro, tokens, half), BF16),
            pltpu.VMEM((2, width, half), BF16),
            pltpu.VMEM((2, 2, rings - 1, chunk, half), BF16),
            pltpu.VMEM((2, chunk, half), BF16),
            pltpu.VMEM((2, 2, share, half), F32),
            pltpu.VMEM((2, share, half), F32),
            pltpu.VMEM((replicas, share, cols), BF16),
            pltpu.VMEM((micro, tokens, width), BF16),
            pltpu.VMEM((micro, tokens, width), BF16),
            pltpu.VMEM((micro, tokens, cols), BF16),
            pltpu.VMEM((replicas, share, cols), F32),
            pltpu.VMEM((replicas, share, cols), F32),
            pltpu.VMEM((sections, final, cols), F32),
            pltpu.VMEM((final, cols), F32),
            dma((3,)),
            dma((micro,)),
            dma((micro,)),
            dma((2,)),
            dma((2,)),
            dma((2, micro)),
            dma((2, micro)),
            dma((2, 2, rings - 1)),
            dma((2, 2, rings - 1)),
            dma((2,)),
            dma((2,)),
            dma((2,)),
            dma((2,)),
            dma((replicas,)),
            dma((replicas,)),
            dma((replicas,)),
            dma((replicas,)),
            dma((sections,)),
            dma(()),
        ],
        compiler_params=pltpu.CompilerParams(
            collective_id=0, has_side_effects=True, vmem_limit_bytes=56 * 1024 * 1024
        ),
    )(
        plan,
        level_index.reshape(1, -1),
        saved_inputs[0],
        norm_gain,
        down_weight[0],
        up_weight[0],
        head_weight,
        head_gain.reshape(1, -1),
        targets,
        levels,
    )
    return grads[None], down_grad[None], up_grad[None], head_grad


def solution(mesh):
    return jax.shard_map(
        functools.partial(local, mesh.shape["section"], mesh.shape["dp"]),
        mesh=mesh,
        in_specs=(
            P("section", None, "dp", None),
            P("section", None),
            P("section", None, None),
            P("section", None, None),
            P("dp", None),
            P(),
            P(None, "dp", None),
            P(),
            P(),
            P(),
        ),
        out_specs=(
            P("section", None, "dp", None),
            P("section", "dp", None),
            P("section", "dp", None),
            P(("section", "dp"), None),
        ),
        check_vma=False,
    )
```

time: 663 us -> 151 us (0.23)
  waiting for transfers between devices: 323 us -> 0 us
  Pallas kernels: 0 us -> 142 us
  matrix products: 135 us -> 0 us
  other arithmetic: 65.3 us -> 0 us
  blocking collectives: 47.3 us -> 0 us
  local copies, waits for them, and re-layouts: 38.1 us -> 7.85 us
  loops' own time: 22.1 us -> 0 us
  between operations: 15.6 us -> 0.64 us
  starting transfers between devices: 14.2 us -> 0 us
    unnamed x3 -> x0, waiting for transfers between devices: 257 us -> none
    pallas_call x0 -> x1, Pallas kernels: none -> 142 us  [local(): pl.pallas_call(functools.partial(body, sections, replicas), out_shape=(ja...]
    dot_general x69 -> x0, matrix products: 135 us -> none  [the longest x11 44.1 us: section_forward(): hidden = jnp.dot(normed, down_local, preferred_element_type=jnp.float32)]
    ppermute x11 -> x0, waiting for transfers between devices: 65.6 us -> none  [passed_along(): lax.ppermute(value, axis, [(source, source + steps) for source in range(i...]
    all_gather x1 -> x0, blocking collectives: 47.3 us -> none  [local(): full_head = lax.all_gather(head_weight, 'dp', axis=0, tiled=True)]
    dynamic_update_slice x33 -> x0, other arithmetic: 42.2 us -> none  [place_slot(): lax.dynamic_update_index_in_dim(store, jnp.where(valid, value, current),...]
    dynamic_slice x66 -> x0, local copies, waits for them, and re-layouts: 28.9 us -> none  [the longest x55 21.3 us: place_slot(): current = lax.dynamic_index_in_dim(store, slot_clip, 0, keepdims=False)]
    another operation x1 -> x0, loops' own time: 22.1 us -> none  [local(): lax.fori_loop(0, micro + sections - 1, functools.partial(tick, with_head=...]
  transfers between devices with their start and end apart: 13 -> 0, of which waited for: 12 -> 0; matrix products, arithmetic and copies ran while one was open for 3% -> 0% of each run, Pallas kernels for 0% -> 0%
where the time goes in v1:
time: 151 us
  Pallas kernels  142 us (94%)
  local copies, waits for them, and re-layouts  7.85 us (5%)
    pallas_call x1, Pallas kernels, local(): pl.pallas_call(functools.partial(body, sections, replicas), out_shape=(ja...  142 us
    unnamed x5, local copies, waits for them, and re-layouts  7.85 us

profile of v1, /device:TPU:1, one launch (start us, length us, event | category | flops | bytes accessed | tf_op | source)
XLA Modules:
  0.0 150.9 jit_solution(12021960354569999161)
XLA Ops:
  0.6 1.4 copy.14.levels_ref
  2.0 142.4 %shard_map.129 = (bf16[4,64,1024]{2,1,0:T(8,128)(2,1)}, f32[32,2048]{1,0:T(8,128)}, f32[32,2048]{1,0:T(8,128)}, f32[4,128]{1,0:T(4,128)}) custom-call(s32[4]{0:T(128)} %plan_ref.1, s32[1,64]{1,0:T(1,128)} %bitcast.15, bf16[4,64,1024]{2,1,0:T(8,128)(2,1)} %bitcast.10, f32[1,1024]{1,0:T(1,128)} %gain_ref.1, bf16[1024,2048]{1,0:T(8,128)(2,1)} %bitcast.8, ...), custom_call_target="tpu_custom_call" | custom-call | tf_op jit(solution)/shard_map/pallas_call | solution.py:581
  144.5 1.9 %copy.19 = bf16[1,4,64,1024]{3,2,1,0:T(8,128)(2,1)} copy(bf16[1,4,64,1024]{3,2,1,0:T(8,128)(2,1)} %bitcast.11) | data formatting | bytes 1048576
  146.3 1.7 %copy.20 = f32[1,32,2048]{2,1,0:T(8,128)} copy(f32[1,32,2048]{2,1,0:T(8,128)} %bitcast.13) | data formatting | bytes 524288
  148.0 1.7 %copy.21 = f32[1,32,2048]{2,1,0:T(8,128)} copy(f32[1,32,2048]{2,1,0:T(8,128)} %bitcast.12) | data formatting | bytes 524288
  149.7 1.3 copy.22

commit v2 on v1

--- a/solution.py
+++ b/solution.py
@@ -88,6 +88,7 @@
     saved,
     down,
     up,
+    down_turned,
     wide,
     inverses,
     normed,
@@ -96,7 +97,9 @@
     cots,
     backs,
     products,
-    ring,
+    early,
+    ring_other,
+    ring_own,
     across,
     halves,
     mates,
@@ -115,6 +118,8 @@
     pair_recv,
     slot_send,
     slot_recv,
+    early_send,
+    early_recv,
     ring_send,
     ring_recv,
     across_send,
@@ -128,11 +133,16 @@
     share_send,
     share_recv,
 ):
-    micro, tokens, width = wide.shape
-    rows_all = micro * tokens
+    units, unit, width = wide.shape
+    micro = saved.shape[0]
+    per_slot = units // micro
+    rows_all = units * unit
     half = active.shape[-1]
     levels = replicas // 4
+    positions = replicas // 2
     chunk = width // (2 * levels)
+    side_rows = width // 2
+    main = ring_other.shape[-1]
     share = width // replicas
     final = head_mine.shape[0]
 
@@ -201,11 +211,14 @@
 
     def norm_slot(slot, unused):
         values = saved[plan_ref[slot]]
-        wide[slot] = values
+        these = pl.ds(slot * per_slot, per_slot)
+        wide[these] = values.reshape(per_slot, unit, width)
         values = values.astype(F32)
         inverse = inverse_rms(values)
-        inverses[slot] = inverse
-        normed[0, slot] = (values * inverse * gain_ref[...]).astype(BF16)
+        inverses[these] = inverse.reshape(per_slot, unit, 1)
+        normed[0, these] = (
+            (values * inverse * gain_ref[...]).astype(BF16).reshape(per_slot, unit, width)
+        )
         return unused
 
     lax.fori_loop(0, micro, norm_slot, 0)
@@ -217,17 +230,36 @@
     )
     pl.semaphore_wait(barrier, heard)
 
+    position = side * levels + level
+
     def gather_copy(offset):
-        peer = lax.rem(me + offset, replicas)
-        return remote(
-            head_ref, full_head.at[me], gather_send.at[offset], gather_recv.at[me], (section, peer)
+        peer = lax.rem(position + offset, positions)
+        return remote(
+            head_ref,
+            full_head.at[position, core],
+            gather_send.at[offset],
+            gather_recv.at[position],
+            (section, peer * 2 + core),
         )
 
     def gather_wait(offset):
-        peer = lax.rem(me + offset, replicas)
+        peer = lax.rem(position + offset, positions)
         remote(
-            head_ref, full_head.at[peer], gather_send.at[offset], gather_recv.at[peer], (section, peer)
+            head_ref,
+            full_head.at[peer, core],
+            gather_send.at[offset],
+            gather_recv.at[peer],
+            (section, peer * 2 + core),
         ).wait_recv()
+
+    def gather_mate(which):
+        return remote(
+            full_head.at[:, which],
+            full_head.at[:, which],
+            gather_send.at[0],
+            gather_recv.at[positions],
+            mate,
+        )
 
     @pl.when(is_last)
     def _():
@@ -235,8 +267,8 @@
             gather_copy(offset).start()
             return unused
 
-        lax.fori_loop(1, replicas, send, 0)
-        full_head[me] = head_ref[...]
+        lax.fori_loop(1, positions, send, 0)
+        full_head[position, core] = head_ref[...]
 
     normed_copy = remote(normed.at[0], normed.at[1], pair_send.at[0], pair_recv.at[0], mate)
     normed_copy.start()
@@ -253,10 +285,10 @@
             hidden = matmul(all_normed, down[:, columns])
             bell = 0.5 * (1.0 + lax.erf(hidden * SQRT_HALF))
             active[where, :, :, inner] = (
-                (hidden * bell).astype(BF16).reshape(micro, tokens, step)
+                (hidden * bell).astype(BF16).reshape(units, unit, step)
             )
             slope = bell + hidden * jnp.exp(-0.5 * hidden * hidden) * INV_SQRT_TAU
-            slopes[part, :, :, inner] = slope.reshape(micro, tokens, step)
+            slopes[part, :, :, inner] = slope.reshape(units, unit, step)
             return unused
 
         lax.fori_loop(0, half // step, forward, 0)
@@ -279,7 +311,7 @@
                     up[columns, part * half : (part + 1) * half],
                     NT,
                 )
-            outputs[:, :, columns] = total.astype(BF16).reshape(micro, tokens, wide_step)
+            outputs[:, :, columns] = total.astype(BF16).reshape(units, unit, wide_step)
             return unused
 
         lax.fori_loop(0, width // wide_step, output_columns, 0)
@@ -288,29 +320,37 @@
             gather_wait(offset)
             return unused
 
-        lax.fori_loop(1, replicas, arrive, 0)
+        lax.fori_loop(1, positions, arrive, 0)
+        gather_mate(core).start()
+        gather_mate(1 - core).wait_recv()
+
+    @pl.when(not_last)
+    def _():
+        turn_step = min(256, width)
+
+        def turn_columns(number, unused):
+            block = pl.ds(pl.multiple_of(number * turn_step, turn_step), turn_step)
+            down_turned[block, :] = down[:, block].T
+            return unused
+
+        lax.fori_loop(0, 2 * half // turn_step, turn_columns, 0)
 
     def head_slot(slot):
-        variables, count = levels_ref.shape
-        diagonal = lax.broadcasted_iota(jnp.int32, (variables, variables), 0) == (
-            lax.broadcasted_iota(jnp.int32, (variables, variables), 1)
-        )
-        threshold = jnp.zeros((1, variables), F32)
-        for number in range(count):
-            row = jnp.sum(
-                jnp.where(diagonal, levels_ref[:, number : number + 1], 0.0), axis=0, keepdims=True
-            )
-            threshold = jnp.where(index_ref[...] == number, row, threshold)
-        head = full_head[...].reshape(width, full_head.shape[2])
-        values = outputs[slot].astype(F32)
+        these = pl.ds(slot * per_slot, per_slot)
+        rows = per_slot * unit
+        choice = lax.broadcasted_iota(jnp.int32, levels_ref.shape, 0) == index_ref[...]
+        threshold = jnp.sum(jnp.where(choice, levels_ref[...], 0.0), axis=0, keepdims=True)
+        head = full_head[...].reshape(width, full_head.shape[3])
+        values = outputs[these].astype(F32).reshape(rows, width)
         inverse = inverse_rms(values)
         head_in = (values * inverse * head_gain_ref[...]).astype(BF16)
-        head_ins[slot] = head_in
+        head_ins[these] = head_in.reshape(per_slot, unit, width)
         predicted = matmul(head_in, head)
         slope = crps_slope(predicted, targets_ref[plan_ref[slot]], threshold).astype(BF16)
-        head_slopes[slot] = slope
+        head_slopes[these] = slope.reshape(per_slot, unit, slope.shape[1])
         upstream = matmul(slope, head, NT)
-        cots[0, slot] = norm_backward(values, inverse, head_gain_ref[...], upstream).astype(BF16)
+        cotangent = norm_backward(values, inverse, head_gain_ref[...], upstream)
+        cots[0, these] = cotangent.astype(BF16).reshape(per_slot, unit, width)
 
     def cot_copy(slot):
         return remote(
@@ -327,36 +367,54 @@
             backs.at[2, slot], backs.at[1, slot], slot_send.at[1, slot], slot_recv.at[1, slot], mate
         )
 
-    def backward(slot, unused):
-        @pl.when(not_last)
-        def _():
-            cot_copy(slot).wait_recv()
-
-        @pl.when(is_last)
-        def _():
-            head_slot(slot)
-
-        pass_cot(slot).start()
-        cotangent = cots[0, slot]
-        back_normed = jnp.zeros((tokens, width), F32)
+    def backward(first, count, turned):
+        these = pl.ds(first, count)
+        rows = count * unit
+        cotangent = cots[0, these].reshape(rows, width)
+        back_normed = jnp.zeros((rows, width), F32)
         for part in range(2):
             columns = slice(part * half, (part + 1) * half)
-            back = (matmul(cotangent, up[:, columns]) * slopes[part, slot]).astype(BF16)
-            backs[2 * lax.rem(core + part, 2), slot] = back
-            back_normed = back_normed + matmul(back, down[:, columns], NT)
-        grads_out[slot] = (
-            cotangent.astype(F32)
-            + norm_backward(wide[slot].astype(F32), inverses[slot], gain_ref[...], back_normed)
-        ).astype(BF16)
+            back_active = matmul(cotangent, up[:, columns])
+            back = (back_active * slopes[part, these].reshape(rows, half)).astype(BF16)
+            backs[2 * lax.rem(core + part, 2), these] = back.reshape(count, unit, half)
+            if turned:
+                back_normed = back_normed + matmul(back, down_turned[columns, :])
+            else:
+                back_normed = back_normed + matmul(back, down[:, columns], NT)
+        values = wide[these].astype(F32).reshape(rows, width)
+        correction = norm_backward(
+            values, inverses[these].reshape(rows, 1), gain_ref[...], back_normed
+        )
+        grads_out[these] = (
+            (cotangent.astype(F32) + correction).astype(BF16).reshape(count, unit, width)
+        )
 
         @pl.when(not_first)
         def _():
-            cot_copy(slot).start()
-
-        pass_back(slot).start()
-        return unused
-
-    lax.fori_loop(0, micro, backward, 0)
+            for number in range(count):
+                cot_copy(first + number).start()
+
+        for number in range(count):
+            pass_cot(first + number).start()
+            pass_back(first + number).start()
+
+    @pl.when(is_last)
+    def _():
+        def from_head(slot, unused):
+            head_slot(slot)
+            backward(slot * per_slot, per_slot, False)
+            return unused
+
+        lax.fori_loop(0, micro, from_head, 0)
+
+    @pl.when(not_last)
+    def _():
+        def from_next(number, unused):
+            cot_copy(number).wait_recv()
+            backward(number, 1, True)
+            return unused
+
+        lax.fori_loop(0, units, from_next, 0)
 
     def slot_arrived(slot, unused):
         pass_cot(slot).wait_recv()
@@ -365,20 +423,93 @@
 
     normed_copy.wait_recv()
     active_copy.wait_recv()
-    lax.fori_loop(0, micro, slot_arrived, 0)
-    row_step = min(256, width)
-
-    def multiply(number, unused):
-        rows = pl.ds(pl.multiple_of(number * row_step, row_step), row_step)
-        for matrix, left, right in ((1, cots, active), (0, normed, backs)):
-            products[matrix, rows] = matmul(
-                left[:, :, :, rows].reshape(2 * rows_all, row_step),
-                right[0:2].reshape(2 * rows_all, half),
-                TN,
-            ).astype(BF16)
-        return unused
-
-    lax.fori_loop(0, width // row_step, multiply, 0)
+    lax.fori_loop(0, units, slot_arrived, 0)
+    row_step = min(256, side_rows)
+
+    def multiply(of_side):
+        def block(number, unused):
+            first = of_side * side_rows + number * row_step
+            rows = pl.ds(pl.multiple_of(first, row_step), row_step)
+            for matrix, left, right in ((1, cots, active), (0, normed, backs)):
+                products[matrix, rows] = matmul(
+                    left[:, :, :, rows].reshape(2 * rows_all, row_step),
+                    right[0:2].reshape(2 * rows_all, half),
+                    TN,
+                ).astype(BF16)
+            return unused
+
+        lax.fori_loop(0, side_rows // row_step, block, 0)
+
+    multiply(1 - side)
+    theirs_rows = pl.ds(pl.multiple_of((1 - side) * side_rows, side_rows), side_rows)
+
+    def early_copy(matrix):
+        return remote(
+            products.at[matrix, theirs_rows, main:half],
+            early.at[matrix],
+            early_send.at[matrix],
+            early_recv.at[matrix],
+            opposite,
+        )
+
+    for matrix in range(2):
+        early_copy(matrix).start()
+
+    longest = levels // 2
+    chains = ((0, 0), (1, 1), (1, 0), (0, 1))
+
+    def hops(matrix, way):
+        return longest if matrix == way else longest - 1
+
+    def rows_of(phase, position):
+        side_of = 1 - side if phase == 0 else side
+        return pl.ds(pl.multiple_of((side_of * levels + position) * chunk, chunk), chunk)
+
+    def ring_rows(phase, matrix, way, hop):
+        left = hops(matrix, way) - hop
+        return rows_of(phase, lax.rem(level + levels + (left if way == 0 else -left), levels))
+
+    def ring_copy(phase, matrix, way, hop):
+        rows = ring_rows(phase, matrix, way, hop)
+        buffer = ring_other if phase == 0 else ring_own
+        source = products.at[matrix, rows, 0:main] if phase == 0 else products.at[matrix, rows]
+        return remote(
+            source,
+            buffer.at[matrix, way, hop],
+            ring_send.at[phase, matrix, way, hop],
+            ring_recv.at[phase, matrix, way, hop],
+            ahead if way == 0 else behind,
+        )
+
+    def ring_start(phase):
+        for matrix, way in chains:
+            ring_copy(phase, matrix, way, 0).start()
+
+    def ring_turns(phase):
+        buffer = ring_other if phase == 0 else ring_own
+        span = buffer.shape[-1]
+        for hop in range(1, longest):
+            for matrix, way in chains:
+                if hop < hops(matrix, way):
+                    ring_copy(phase, matrix, way, hop - 1).wait_recv()
+                    rows = ring_rows(phase, matrix, way, hop)
+                    total = products[matrix, rows, 0:span].astype(F32) + (
+                        buffer[matrix, way, hop - 1].astype(F32)
+                    )
+                    products[matrix, rows, 0:span] = total.astype(BF16)
+                    ring_copy(phase, matrix, way, hop).start()
+
+    def ring_total(phase, matrix):
+        buffer = ring_other if phase == 0 else ring_own
+        total = products[matrix, rows_of(phase, level), 0 : buffer.shape[-1]].astype(F32)
+        for way in (1, 0) if matrix == 0 else (0, 1):
+            last = hops(matrix, way) - 1
+            ring_copy(phase, matrix, way, last).wait_recv()
+            total = total + buffer[matrix, way, last].astype(F32)
+        return total
+
+    ring_start(0)
+    multiply(side)
 
     def term_copy(offset):
         peer = lax.rem(me + offset, replicas)
@@ -412,46 +543,25 @@
 
         lax.fori_loop(1, replicas, send, 0)
 
-    def place(matrix, turn):
-        if matrix == 0:
-            return lax.rem(level + 2 * levels - 1 - turn, levels)
-        return lax.rem(level + 1 + turn, levels)
-
-    def rows_of(which, position):
-        side_of = 1 - side if which == 0 else side
-        return pl.ds(pl.multiple_of((side_of * levels + position) * chunk, chunk), chunk)
-
-    def ring_copy(matrix, which, turn):
-        return remote(
-            products.at[matrix, rows_of(which, place(matrix, turn))],
-            ring.at[matrix, which, turn],
-            ring_send.at[matrix, which, turn],
-            ring_recv.at[matrix, which, turn],
-            ahead if matrix == 0 else behind,
-        )
-
-    def add_arrived(matrix, which, turn):
-        ring_copy(matrix, which, turn - 1).wait_recv()
-        rows = rows_of(which, place(matrix, turn))
-        return products[matrix, rows].astype(F32) + ring[matrix, which, turn - 1].astype(F32)
-
-    for which in range(2):
-        for matrix in range(2):
-            ring_copy(matrix, which, 0).start()
-
-    def turn_ring(turn, unused):
-        for which in range(2):
-            for matrix in range(2):
-                rows = rows_of(which, place(matrix, turn))
-                products[matrix, rows] = add_arrived(matrix, which, turn).astype(BF16)
-                ring_copy(matrix, which, turn).start()
-        return unused
-
-    lax.fori_loop(1, levels - 1, turn_ring, 0)
+    ring_turns(0)
+    for matrix in range(2):
+        early_copy(matrix).wait_recv()
+
+        def add_early(number, unused, matrix=matrix):
+            rows = pl.ds(pl.multiple_of(side * side_rows + number * chunk, chunk), chunk)
+            from_rows = pl.ds(pl.multiple_of(number * chunk, chunk), chunk)
+            total = products[matrix, rows, main:half].astype(F32) + (
+                early[matrix, from_rows].astype(F32)
+            )
+            products[matrix, rows, main:half] = total.astype(BF16)
+            return unused
+
+        lax.fori_loop(0, levels, add_early, 0)
+    ring_start(1)
 
     def across_copy(matrix):
         return remote(
-            products.at[matrix, rows_of(0, level)],
+            products.at[matrix, rows_of(0, level), 0:main],
             across.at[matrix],
             across_send.at[matrix],
             across_recv.at[matrix],
@@ -459,8 +569,9 @@
         )
 
     for matrix in range(2):
-        products[matrix, rows_of(0, level)] = add_arrived(matrix, 0, levels - 1).astype(BF16)
+        products[matrix, rows_of(0, level), 0:main] = ring_total(0, matrix).astype(BF16)
         across_copy(matrix).start()
+    ring_turns(1)
 
     def mate_copy(matrix):
         return remote(
@@ -470,10 +581,11 @@
     mine = pl.ds(pl.multiple_of(core * half, half), half)
     theirs = pl.ds(pl.multiple_of((1 - core) * half, half), half)
     for matrix, result in ((0, down_out), (1, up_out)):
-        total = add_arrived(matrix, 1, levels - 1)
+        total = ring_total(1, matrix) / LOSS_SCALE
         across_copy(matrix).wait_recv()
-        total = (total + across[matrix].astype(F32)) / LOSS_SCALE
-        halves[matrix] = total.reshape(2, share, half)
+        other = across[matrix].astype(F32) / LOSS_SCALE
+        halves[matrix, :, :, 0:main] = (total[:, 0:main] + other).reshape(2, share, main)
+        halves[matrix, :, :, main:half] = total[:, main:half].reshape(2, share, half - main)
         mate_copy(matrix).start()
         result[:, mine] = halves[matrix, core]
 
@@ -516,7 +628,7 @@
         pass_back(slot).wait_send()
         return unused
 
-    lax.fori_loop(0, micro, slot_left, 0)
+    lax.fori_loop(0, units, slot_left, 0)
 
     @pl.when(not_first)
     def _():
@@ -524,33 +636,49 @@
             cot_copy(slot).wait_send()
             return unused
 
-        lax.fori_loop(0, micro, cot_left, 0)
-
-    def ring_left(turn, unused):
-        for which in range(2):
-            for matrix in range(2):
-                ring_copy(matrix, which, turn).wait_send()
-        return unused
-
-    lax.fori_loop(0, levels - 1, ring_left, 0)
+        lax.fori_loop(0, units, cot_left, 0)
+
+    for phase in range(2):
+        for matrix, way in chains:
+            for hop in range(hops(matrix, way)):
+                ring_copy(phase, matrix, way, hop).wait_send()
     for matrix in range(2):
+        early_copy(matrix).wait_send()
         across_copy(matrix).wait_send()
         mate_copy(matrix).wait_send()
 
     @pl.when(is_last)
     def _():
         def head_left(offset, unused):
+            term_copy(offset).wait_send()
+            return unused
+
+        lax.fori_loop(1, replicas, head_left, 0)
+
+        def gather_left(offset, unused):
             gather_copy(offset).wait_send()
-            term_copy(offset).wait_send()
-            return unused
-
-        lax.fori_loop(1, replicas, head_left, 0)
+            return unused
+
+        lax.fori_loop(1, positions, gather_left, 0)
+        gather_mate(core).wait_send()
         for number in range(sections):
             block, copy = share_copy(number)
 
             @pl.when(block != (sections - 1) * replicas + me)
             def _():
                 copy.wait_send()
+
+
+def hand_out(*refs):
+    sources, results, sem = refs[:4], refs[4:8], refs[8]
+    copies = [
+        pltpu.make_async_copy(source, result, sem.at[number])
+        for number, (source, result) in enumerate(zip(sources, results))
+    ]
+    for copy in copies:
+        copy.start()
+    for copy in copies:
+        copy.wait()
 
 
 def local(
@@ -575,13 +703,17 @@
     chunk = width // (2 * rings)
     share = width // replicas
     final = share // sections
+    unit = tokens // 2
+    units_all = 2 * micro
+    main = half - half // 4
+    longest = rings // 2
     whole = pl.BlockSpec(memory_space=pltpu.VMEM)
     anywhere = pl.BlockSpec(memory_space=pl.ANY)
     dma = pltpu.SemaphoreType.DMA
     grads, down_grad, up_grad, head_grad = pl.pallas_call(
         functools.partial(body, sections, replicas),
         out_shape=(
-            jax.ShapeDtypeStruct((micro, tokens, width), BF16),
+            jax.ShapeDtypeStruct((units_all, unit, width), BF16),
             jax.ShapeDtypeStruct((share, units), F32),
             jax.ShapeDtypeStruct((share, units), F32),
             jax.ShapeDtypeStruct((final, cols), F32),
@@ -603,41 +735,46 @@
             pltpu.VMEM((micro, tokens, width), BF16),
             pltpu.VMEM((width, units), BF16),
             pltpu.VMEM((width, units), BF16),
-            pltpu.VMEM((micro, tokens, width), BF16),
-            pltpu.VMEM((micro, tokens, 1), F32),
-            pltpu.VMEM((2, micro, tokens, width), BF16),
-            pltpu.VMEM((3, micro, tokens, half), BF16),
-            pltpu.VMEM((2, micro, tokens, half), F32),
-            pltpu.VMEM((2, micro, tokens, width), BF16),
-            pltpu.VMEM((3, micro, tokens, half), BF16),
+            pltpu.VMEM((units, width), BF16),
+            pltpu.VMEM((units_all, unit, width), BF16),
+            pltpu.VMEM((units_all, unit, 1), F32),
+            pltpu.VMEM((2, units_all, unit, width), BF16),
+            pltpu.VMEM((3, units_all, unit, half), BF16),
+            pltpu.VMEM((2, units_all, unit, half), F32),
+            pltpu.VMEM((2, units_all, unit, width), BF16),
+            pltpu.VMEM((3, units_all, unit, half), BF16),
             pltpu.VMEM((2, width, half), BF16),
-            pltpu.VMEM((2, 2, rings - 1, chunk, half), BF16),
-            pltpu.VMEM((2, chunk, half), BF16),
+            pltpu.VMEM((2, width // 2, half - main), BF16),
+            pltpu.VMEM((2, 2, longest, chunk, main), BF16),
+            pltpu.VMEM((2, 2, longest, chunk, half), BF16),
+            pltpu.VMEM((2, chunk, main), BF16),
             pltpu.VMEM((2, 2, share, half), F32),
             pltpu.VMEM((2, share, half), F32),
-            pltpu.VMEM((replicas, share, cols), BF16),
-            pltpu.VMEM((micro, tokens, width), BF16),
-            pltpu.VMEM((micro, tokens, width), BF16),
-            pltpu.VMEM((micro, tokens, cols), BF16),
+            pltpu.VMEM((replicas // 2, 2, share, cols), BF16),
+            pltpu.VMEM((units_all, unit, width), BF16),
+            pltpu.VMEM((units_all, unit, width), BF16),
+            pltpu.VMEM((units_all, unit, cols), BF16),
             pltpu.VMEM((replicas, share, cols), F32),
             pltpu.VMEM((replicas, share, cols), F32),
             pltpu.VMEM((sections, final, cols), F32),
             pltpu.VMEM((final, cols), F32),
             dma((3,)),
-            dma((micro,)),
-            dma((micro,)),
+            dma((units_all,)),
+            dma((units_all,)),
             dma((2,)),
             dma((2,)),
-            dma((2, micro)),
-            dma((2, micro)),
-            dma((2, 2, rings - 1)),
-            dma((2, 2, rings - 1)),
+            dma((2, units_all)),
+            dma((2, units_all)),
+            dma((2,)),
+            dma((2,)),
+            dma((2, 2, 2, longest)),
+            dma((2, 2, 2, longest)),
             dma((2,)),
             dma((2,)),
             dma((2,)),
             dma((2,)),
-            dma((replicas,)),
-            dma((replicas,)),
+            dma((replicas // 2,)),
+            dma((replicas // 2 + 1,)),
             dma((replicas,)),
             dma((replicas,)),
             dma((sections,)),
@@ -656,9 +793,19 @@
         head_weight,
         head_gain.reshape(1, -1),
         targets,
-        levels,
+        levels.T,
     )
-    return grads[None], down_grad[None], up_grad[None], head_grad
+    grads, down_grad, up_grad, head_grad = pl.pallas_call(
+        hand_out,
+        out_shape=tuple(
+            jax.ShapeDtypeStruct(value.shape, value.dtype)
+            for value in (grads, down_grad, up_grad, head_grad)
+        ),
+        in_specs=[anywhere] * 4,
+        out_specs=(anywhere,) * 4,
+        scratch_shapes=[dma((4,))],
+    )(grads, down_grad, up_grad, head_grad)
+    return grads.reshape(1, micro, tokens, width), down_grad[None], up_grad[None], head_grad
 
 
 def solution(mesh):

time: 151 us -> 155 us (1.026)
  Pallas kernels: 142 us -> 154 us
  local copies, waits for them, and re-layouts: 7.85 us -> 0 us
    pallas_call x0 -> x1, Pallas kernels: none -> 33 us  [local(): pl.pallas_call(hand_out, out_shape=tuple((jax.ShapeDtypeStruct(value.shap...]
    pallas_call x1, Pallas kernels: 142 us -> 121 us  [local(): pl.pallas_call(functools.partial(body, sections, replicas), out_shape=(ja...]
    unnamed x5 -> x0, local copies, waits for them, and re-layouts: 7.85 us -> none
where the time goes in v2:
time: 155 us
  Pallas kernels  154 us (99%)
    pallas_call x1, Pallas kernels, local(): pl.pallas_call(functools.partial(body, sections, replicas), out_shape=(ja...  121 us
    pallas_call x1, Pallas kernels, local(): pl.pallas_call(hand_out, out_shape=tuple((jax.ShapeDtypeStruct(value.shap...  33 us

profile of v2, /device:TPU:1, one launch (start us, length us, event | category | flops | bytes accessed | tf_op | source)
XLA Modules:
  0.0 155.1 jit_solution(17402332475898447305)
XLA Ops:
  0.6 121.5 %shard_map.129 = (bf16[8,32,1024]{2,1,0:T(8,128)(2,1)}, f32[32,2048]{1,0:T(8,128)}, f32[32,2048]{1,0:T(8,128)}, f32[4,128]{1,0:T(4,128)}) custom-call(s32[4]{0:T(128)} %plan_ref.1, s32[1,64]{1,0:T(1,128)} %bitcast.14, bf16[4,64,1024]{2,1,0:T(8,128)(2,1)} %bitcast.11, f32[1,1024]{1,0:T(1,128)} %gain_ref.1, bf16[1024,2048]{1,0:T(8,128)(2,1)} %bitcast.9, ...), custom_call_target="tpu_custom_call" | custom-call | tf_op jit(solution)/shard_map/pallas_call | solution.py:713
  122.1 33.0 %shard_map.130 = (bf16[8,32,1024]{2,1,0:T(8,128)(2,1)}, f32[32,2048]{1,0:T(8,128)}, f32[32,2048]{1,0:T(8,128)}, f32[4,128]{1,0:T(4,128)}) custom-call(bf16[8,32,1024]{2,1,0:T(8,128)(2,1)} %get-tuple-element.12.refs_0_, f32[32,2048]{1,0:T(8,128)} %get-tuple-element.13.refs_1_, f32[32,2048]{1,0:T(8,128)} %get-tuple-element.14.refs_2_, ...), custom_call_target="tpu_custom_call" | custom-call | tf_op jit(solution)/shard_map/pallas_call | solution.py:798

commit v3 on v2

--- a/solution.py
+++ b/solution.py
@@ -670,14 +670,21 @@
 
 
 def hand_out(*refs):
-    sources, results, sem = refs[:4], refs[4:8], refs[8]
-    copies = [
-        pltpu.make_async_copy(source, result, sem.at[number])
-        for number, (source, result) in enumerate(zip(sources, results))
+    sources, results, held, sem = refs[:4], refs[4:8], refs[8:12], refs[12]
+    incoming = [
+        pltpu.make_async_copy(source, middle, sem.at[0, number])
+        for number, (source, middle) in enumerate(zip(sources, held))
     ]
-    for copy in copies:
+    outgoing = [
+        pltpu.make_async_copy(middle, result, sem.at[1, number])
+        for number, (middle, result) in enumerate(zip(held, results))
+    ]
+    for copy in incoming:
         copy.start()
-    for copy in copies:
+    for arrival, copy in zip(incoming, outgoing):
+        arrival.wait()
+        copy.start()
+    for copy in outgoing:
         copy.wait()
 
 
@@ -803,7 +810,11 @@
         ),
         in_specs=[anywhere] * 4,
         out_specs=(anywhere,) * 4,
-        scratch_shapes=[dma((4,))],
+        scratch_shapes=[
+            pltpu.VMEM(value.shape, value.dtype)
+            for value in (grads, down_grad, up_grad, head_grad)
+        ]
+        + [dma((2, 4))],
     )(grads, down_grad, up_grad, head_grad)
     return grads.reshape(1, micro, tokens, width), down_grad[None], up_grad[None], head_grad
 

time: 155 us -> 124 us (0.80)
  Pallas kernels: 154 us -> 124 us
    pallas_call x1, Pallas kernels: 33 us -> 2.08 us  [local(): pl.pallas_call(hand_out, out_shape=tuple((jax.ShapeDtypeStruct(value.shap...]
where the time goes in v3:
time: 124 us
  Pallas kernels  124 us (100%)
    pallas_call x1, Pallas kernels, local(): pl.pallas_call(functools.partial(body, sections, replicas), out_shape=(ja...  121 us

profile of v3, /device:TPU:1, one launch (start us, length us, event | category | flops | bytes accessed | tf_op | source)
XLA Modules:
  0.0 124.2 jit_solution(13302977317615482983)
XLA Ops:
  0.6 121.5 %shard_map.129 = (bf16[8,32,1024]{2,1,0:T(8,128)(2,1)}, f32[32,2048]{1,0:T(8,128)}, f32[32,2048]{1,0:T(8,128)}, f32[4,128]{1,0:T(4,128)}) custom-call(s32[4]{0:T(128)} %plan_ref.1, s32[1,64]{1,0:T(1,128)} %bitcast.14, bf16[4,64,1024]{2,1,0:T(8,128)(2,1)} %bitcast.11, f32[1,1024]{1,0:T(1,128)} %gain_ref.1, bf16[1024,2048]{1,0:T(8,128)(2,1)} %bitcast.9, ...), custom_call_target="tpu_custom_call" | custom-call | tf_op jit(solution)/shard_map/pallas_call | solution.py:720
  122.1 2.1 %shard_map.130 = (bf16[8,32,1024]{2,1,0:T(8,128)(2,1)}, f32[32,2048]{1,0:T(8,128)}, f32[32,2048]{1,0:T(8,128)}, f32[4,128]{1,0:T(4,128)}) custom-call(bf16[8,32,1024]{2,1,0:T(8,128)(2,1)} %get-tuple-element.12.refs_0_, f32[32,2048]{1,0:T(8,128)} %get-tuple-element.13.refs_1_, f32[32,2048]{1,0:T(8,128)} %get-tuple-element.14.refs_2_, ...), custom_call_target="tpu_custom_call" | custom-call | tf_op jit(solution)/shard_map/pallas_call | solution.py:805

commit v4 on v3

--- a/solution.py
+++ b/solution.py
@@ -94,12 +94,14 @@
     normed,
     active,
     slopes,
+    hiddens,
     cots,
     backs,
+    grads,
     products,
     early,
-    ring_other,
-    ring_own,
+    ring_main,
+    ring_early,
     across,
     halves,
     mates,
@@ -142,7 +144,8 @@
     positions = replicas // 2
     chunk = width // (2 * levels)
     side_rows = width // 2
-    main = ring_other.shape[-1]
+    main = ring_main.shape[-1]
+    column_half = width // 2
     share = width // replicas
     final = head_mine.shape[0]
 
@@ -289,6 +292,7 @@
             )
             slope = bell + hidden * jnp.exp(-0.5 * hidden * hidden) * INV_SQRT_TAU
             slopes[part, :, :, inner] = slope.reshape(units, unit, step)
+            hiddens[part, :, :, inner] = hidden.reshape(units, unit, step)
             return unused
 
         lax.fori_loop(0, half // step, forward, 0)
@@ -316,6 +320,17 @@
 
         lax.fori_loop(0, width // wide_step, output_columns, 0)
 
+    turn_step = min(256, width)
+
+    def turn_columns(number, unused):
+        block = pl.ds(pl.multiple_of(number * turn_step, turn_step), turn_step)
+        down_turned[block, :] = down[:, block].T
+        return unused
+
+    lax.fori_loop(0, 2 * half // turn_step, turn_columns, 0)
+
+    @pl.when(is_last)
+    def _():
         def arrive(offset, unused):
             gather_wait(offset)
             return unused
@@ -323,17 +338,6 @@
         lax.fori_loop(1, positions, arrive, 0)
         gather_mate(core).start()
         gather_mate(1 - core).wait_recv()
-
-    @pl.when(not_last)
-    def _():
-        turn_step = min(256, width)
-
-        def turn_columns(number, unused):
-            block = pl.ds(pl.multiple_of(number * turn_step, turn_step), turn_step)
-            down_turned[block, :] = down[:, block].T
-            return unused
-
-        lax.fori_loop(0, 2 * half // turn_step, turn_columns, 0)
 
     def head_slot(slot):
         these = pl.ds(slot * per_slot, per_slot)
@@ -352,9 +356,14 @@
         cotangent = norm_backward(values, inverse, head_gain_ref[...], upstream)
         cots[0, these] = cotangent.astype(BF16).reshape(per_slot, unit, width)
 
-    def cot_copy(slot):
+    def cot_copy(slot, piece):
+        columns = slice(piece * column_half, (piece + 1) * column_half)
         return remote(
-            grads_out.at[slot], cots.at[0, slot], cot_send.at[slot], cot_recv.at[slot], receiver
+            grads.at[slot, :, columns],
+            cots.at[0, slot, :, columns],
+            cot_send.at[slot, piece],
+            cot_recv.at[slot, piece],
+            receiver,
         )
 
     def pass_cot(slot):
@@ -367,32 +376,44 @@
             backs.at[2, slot], backs.at[1, slot], slot_send.at[1, slot], slot_recv.at[1, slot], mate
         )
 
-    def backward(first, count, turned):
+    def backward(first, count, arriving):
         these = pl.ds(first, count)
         rows = count * unit
-        cotangent = cots[0, these].reshape(rows, width)
-        back_normed = jnp.zeros((rows, width), F32)
+        back_active = None
+        for piece in range(2):
+            if arriving:
+                cot_copy(first, piece).wait_recv()
+            columns = slice(piece * column_half, (piece + 1) * column_half)
+            part = matmul(cots[0, these, :, columns].reshape(rows, column_half), up[columns, :])
+            back_active = part if back_active is None else back_active + part
+        dot = jnp.zeros((rows, 1), F32)
+        back_parts = []
         for part in range(2):
             columns = slice(part * half, (part + 1) * half)
-            back_active = matmul(cotangent, up[:, columns])
-            back = (back_active * slopes[part, these].reshape(rows, half)).astype(BF16)
+            back = (back_active[:, columns] * slopes[part, these].reshape(rows, half)).astype(BF16)
             backs[2 * lax.rem(core + part, 2), these] = back.reshape(count, unit, half)
-            if turned:
-                back_normed = back_normed + matmul(back, down_turned[columns, :])
-            else:
-                back_normed = back_normed + matmul(back, down[:, columns], NT)
-        values = wide[these].astype(F32).reshape(rows, width)
-        correction = norm_backward(
-            values, inverses[these].reshape(rows, 1), gain_ref[...], back_normed
-        )
-        grads_out[these] = (
-            (cotangent.astype(F32) + correction).astype(BF16).reshape(count, unit, width)
-        )
-
-        @pl.when(not_first)
-        def _():
-            for number in range(count):
-                cot_copy(first + number).start()
+            dot = dot + jnp.sum(
+                back.astype(F32) * hiddens[part, these].reshape(rows, half), axis=-1, keepdims=True
+            )
+            back_parts.append(back)
+        inverse = inverses[these].reshape(rows, 1)
+        pull = inverse * inverse * dot * (1.0 / width)
+        for piece in range(2):
+            columns = slice(piece * column_half, (piece + 1) * column_half)
+            back_normed = matmul(back_parts[0], down_turned[0:half, columns]) + matmul(
+                back_parts[1], down_turned[half : 2 * half, columns]
+            )
+            grad = (
+                cots[0, these, :, columns].astype(F32).reshape(rows, column_half)
+                + inverse * (gain_ref[:, columns] * back_normed)
+                - wide[these, :, columns].astype(F32).reshape(rows, column_half) * pull
+            )
+            grads[these, :, columns] = grad.astype(BF16).reshape(count, unit, column_half)
+
+            @pl.when(not_first)
+            def _():
+                for number in range(count):
+                    cot_copy(first + number, piece).start()
 
         for number in range(count):
             pass_cot(first + number).start()
@@ -410,37 +431,31 @@
     @pl.when(not_last)
     def _():
         def from_next(number, unused):
-            cot_copy(number).wait_recv()
             backward(number, 1, True)
             return unused
 
         lax.fori_loop(0, units, from_next, 0)
 
-    def slot_arrived(slot, unused):
-        pass_cot(slot).wait_recv()
-        pass_back(slot).wait_recv()
-        return unused
-
-    normed_copy.wait_recv()
-    active_copy.wait_recv()
-    lax.fori_loop(0, units, slot_arrived, 0)
+    grads_copy = pltpu.make_async_copy(grads, grads_out, load_sem.at[3])
+    grads_copy.start()
+
     row_step = min(256, side_rows)
 
-    def multiply(of_side):
+    def multiply(matrix, of_side):
+        left, right = (normed, backs) if matrix == 0 else (cots, active)
+
         def block(number, unused):
             first = of_side * side_rows + number * row_step
             rows = pl.ds(pl.multiple_of(first, row_step), row_step)
-            for matrix, left, right in ((1, cots, active), (0, normed, backs)):
-                products[matrix, rows] = matmul(
-                    left[:, :, :, rows].reshape(2 * rows_all, row_step),
-                    right[0:2].reshape(2 * rows_all, half),
-                    TN,
-                ).astype(BF16)
+            products[matrix, rows] = matmul(
+                left[:, :, :, rows].reshape(2 * rows_all, row_step),
+                right[0:2].reshape(2 * rows_all, half),
+                TN,
+            ).astype(BF16)
             return unused
 
         lax.fori_loop(0, side_rows // row_step, block, 0)
 
-    multiply(1 - side)
     theirs_rows = pl.ds(pl.multiple_of((1 - side) * side_rows, side_rows), side_rows)
 
     def early_copy(matrix):
@@ -452,11 +467,11 @@
             opposite,
         )
 
-    for matrix in range(2):
-        early_copy(matrix).start()
-
     longest = levels // 2
-    chains = ((0, 0), (1, 1), (1, 0), (0, 1))
+    phase_columns = (slice(0, main), slice(0, main), slice(main, half))
+
+    def buffer_of(phase):
+        return ring_early if phase == 2 else ring_main.at[phase]
 
     def hops(matrix, way):
         return longest if matrix == way else longest - 1
@@ -470,84 +485,45 @@
         return rows_of(phase, lax.rem(level + levels + (left if way == 0 else -left), levels))
 
     def ring_copy(phase, matrix, way, hop):
-        rows = ring_rows(phase, matrix, way, hop)
-        buffer = ring_other if phase == 0 else ring_own
-        source = products.at[matrix, rows, 0:main] if phase == 0 else products.at[matrix, rows]
         return remote(
-            source,
-            buffer.at[matrix, way, hop],
+            products.at[matrix, ring_rows(phase, matrix, way, hop), phase_columns[phase]],
+            buffer_of(phase).at[matrix, way, hop],
             ring_send.at[phase, matrix, way, hop],
             ring_recv.at[phase, matrix, way, hop],
             ahead if way == 0 else behind,
         )
 
-    def ring_start(phase):
-        for matrix, way in chains:
+    def ways_of(matrix):
+        return (0, 1) if matrix == 0 else (1, 0)
+
+    def ring_start(phase, matrix):
+        for way in ways_of(matrix):
             ring_copy(phase, matrix, way, 0).start()
 
-    def ring_turns(phase):
-        buffer = ring_other if phase == 0 else ring_own
-        span = buffer.shape[-1]
-        for hop in range(1, longest):
-            for matrix, way in chains:
-                if hop < hops(matrix, way):
-                    ring_copy(phase, matrix, way, hop - 1).wait_recv()
-                    rows = ring_rows(phase, matrix, way, hop)
-                    total = products[matrix, rows, 0:span].astype(F32) + (
-                        buffer[matrix, way, hop - 1].astype(F32)
-                    )
-                    products[matrix, rows, 0:span] = total.astype(BF16)
-                    ring_copy(phase, matrix, way, hop).start()
+    def ring_turn(phase, matrix, hop):
+        columns = phase_columns[phase]
+        for way in ways_of(matrix):
+            if 0 < hop < hops(matrix, way):
+                ring_copy(phase, matrix, way, hop - 1).wait_recv()
+                rows = ring_rows(phase, matrix, way, hop)
+                total = products[matrix, rows, columns].astype(F32) + (
+                    buffer_of(phase)[matrix, way, hop - 1].astype(F32)
+                )
+                products[matrix, rows, columns] = total.astype(BF16)
+                ring_copy(phase, matrix, way, hop).start()
 
     def ring_total(phase, matrix):
-        buffer = ring_other if phase == 0 else ring_own
-        total = products[matrix, rows_of(phase, level), 0 : buffer.shape[-1]].astype(F32)
-        for way in (1, 0) if matrix == 0 else (0, 1):
+        total = products[matrix, rows_of(phase, level), phase_columns[phase]].astype(F32)
+        for way in reversed(ways_of(matrix)):
             last = hops(matrix, way) - 1
             ring_copy(phase, matrix, way, last).wait_recv()
-            total = total + buffer[matrix, way, last].astype(F32)
+            total = total + buffer_of(phase)[matrix, way, last].astype(F32)
         return total
 
-    ring_start(0)
-    multiply(side)
-
-    def term_copy(offset):
-        peer = lax.rem(me + offset, replicas)
-        return remote(
-            head_parts.at[peer], head_terms.at[me], term_send.at[offset], term_recv.at[me], (section, peer)
-        )
-
-    def term_wait(offset):
-        peer = lax.rem(me + offset, replicas)
-        remote(
-            head_parts.at[peer], head_terms.at[peer], term_send.at[offset], term_recv.at[peer], (section, peer)
-        ).wait_recv()
-
-    def share_copy(number):
-        block = sections * me + number
-        target = (lax.div(block, replicas), lax.rem(block, replicas))
-        return block, remote(head_sums.at[number], head_mine, share_send.at[number], share_recv, target)
-
-    @pl.when(is_last)
-    def _():
-        part = matmul(
-            head_ins[...].reshape(rows_all, width),
-            head_slopes[...].reshape(rows_all, head_slopes.shape[2]),
-            TN,
-        )
-        head_parts[...] = part.reshape(head_parts.shape)
-
-        def send(offset, unused):
-            term_copy(offset).start()
-            return unused
-
-        lax.fori_loop(1, replicas, send, 0)
-
-    ring_turns(0)
-    for matrix in range(2):
+    def add_early(matrix):
         early_copy(matrix).wait_recv()
 
-        def add_early(number, unused, matrix=matrix):
+        def add(number, unused):
             rows = pl.ds(pl.multiple_of(side * side_rows + number * chunk, chunk), chunk)
             from_rows = pl.ds(pl.multiple_of(number * chunk, chunk), chunk)
             total = products[matrix, rows, main:half].astype(F32) + (
@@ -556,8 +532,62 @@
             products[matrix, rows, main:half] = total.astype(BF16)
             return unused
 
-        lax.fori_loop(0, levels, add_early, 0)
-    ring_start(1)
+        lax.fori_loop(0, levels, add, 0)
+
+    def cot_passed(number, unused):
+        pass_cot(number).wait_recv()
+        return unused
+
+    def back_passed(number, unused):
+        pass_back(number).wait_recv()
+        return unused
+
+    normed_copy.wait_recv()
+    active_copy.wait_recv()
+    lax.fori_loop(0, units, cot_passed, 0)
+    multiply(1, 1 - side)
+    early_copy(1).start()
+    ring_start(0, 1)
+    lax.fori_loop(0, units, back_passed, 0)
+    multiply(0, 1 - side)
+    early_copy(0).start()
+    ring_start(0, 0)
+    multiply(1, side)
+    ring_start(1, 1)
+    multiply(0, side)
+    ring_start(1, 0)
+
+    def term_copy(offset):
+        peer = lax.rem(me + offset, replicas)
+        return remote(
+            head_parts.at[peer], head_terms.at[me], term_send.at[offset], term_recv.at[me], (section, peer)
+        )
+
+    def term_wait(offset):
+        peer = lax.rem(me + offset, replicas)
+        remote(
+            head_parts.at[peer], head_terms.at[peer], term_send.at[offset], term_recv.at[peer], (section, peer)
+        ).wait_recv()
+
+    def share_copy(number):
+        block = sections * me + number
+        target = (lax.div(block, replicas), lax.rem(block, replicas))
+        return block, remote(head_sums.at[number], head_mine, share_send.at[number], share_recv, target)
+
+    @pl.when(is_last)
+    def _():
+        part = matmul(
+            head_ins[...].reshape(rows_all, width),
+            head_slopes[...].reshape(rows_all, head_slopes.shape[2]),
+            TN,
+        )
+        head_parts[...] = part.reshape(head_parts.shape)
+
+        def send(offset, unused):
+            term_copy(offset).start()
+            return unused
+
+        lax.fori_loop(1, replicas, send, 0)
 
     def across_copy(matrix):
         return remote(
@@ -568,10 +598,32 @@
             opposite,
         )
 
-    for matrix in range(2):
+    for hop in range(1, longest):
+        for phase in (0, 1):
+            for matrix in (1, 0):
+                ring_turn(phase, matrix, hop)
+        if hop == 1:
+            add_early(1)
+            ring_start(2, 1)
+        elif hop == 2:
+            add_early(0)
+            ring_start(2, 0)
+            ring_turn(2, 1, 1)
+        elif hop == 3:
+            ring_turn(2, 0, 1)
+            ring_turn(2, 1, 2)
+    if longest < 3:
+        add_early(0)
+        ring_start(2, 0)
+        ring_turn(2, 1, 1)
+        ring_turn(2, 0, 1)
+    for matrix in (1, 0):
         products[matrix, rows_of(0, level), 0:main] = ring_total(0, matrix).astype(BF16)
         across_copy(matrix).start()
-    ring_turns(1)
+    if longest >= 3:
+        ring_turn(2, 0, 2)
+        ring_turn(2, 1, 3)
+        ring_turn(2, 0, 3)
 
     def mate_copy(matrix):
         return remote(
@@ -580,12 +632,14 @@
 
     mine = pl.ds(pl.multiple_of(core * half, half), half)
     theirs = pl.ds(pl.multiple_of((1 - core) * half, half), half)
-    for matrix, result in ((0, down_out), (1, up_out)):
-        total = ring_total(1, matrix) / LOSS_SCALE
+    for matrix in (1, 0):
+        total = ring_total(1, matrix)
         across_copy(matrix).wait_recv()
-        other = across[matrix].astype(F32) / LOSS_SCALE
-        halves[matrix, :, :, 0:main] = (total[:, 0:main] + other).reshape(2, share, main)
-        halves[matrix, :, :, main:half] = total[:, main:half].reshape(2, share, half - main)
+        total = (total + across[matrix].astype(F32)) / LOSS_SCALE
+        halves[matrix, :, :, 0:main] = total.reshape(2, share, main)
+    for matrix, result in ((1, up_out), (0, down_out)):
+        total = ring_total(2, matrix) / LOSS_SCALE
+        halves[matrix, :, :, main:half] = total.reshape(2, share, half - main)
         mate_copy(matrix).start()
         result[:, mine] = halves[matrix, core]
 
@@ -620,6 +674,7 @@
 
     head_out[...] = head_mine[...]
 
+    grads_copy.wait()
     normed_copy.wait_send()
     active_copy.wait_send()
 
@@ -633,15 +688,17 @@
     @pl.when(not_first)
     def _():
         def cot_left(slot, unused):
-            cot_copy(slot).wait_send()
+            cot_copy(slot, 0).wait_send()
+            cot_copy(slot, 1).wait_send()
             return unused
 
         lax.fori_loop(0, units, cot_left, 0)
 
-    for phase in range(2):
-        for matrix, way in chains:
-            for hop in range(hops(matrix, way)):
-                ring_copy(phase, matrix, way, hop).wait_send()
+    for phase in range(3):
+        for matrix in range(2):
+            for way in range(2):
+                for hop in range(hops(matrix, way)):
+                    ring_copy(phase, matrix, way, hop).wait_send()
     for matrix in range(2):
         early_copy(matrix).wait_send()
         across_copy(matrix).wait_send()
@@ -737,7 +794,7 @@
             whole,
             whole,
         ],
-        out_specs=(whole, whole, whole, whole),
+        out_specs=(anywhere, whole, whole, whole),
         scratch_shapes=[
             pltpu.VMEM((micro, tokens, width), BF16),
             pltpu.VMEM((width, units), BF16),
@@ -748,12 +805,14 @@
             pltpu.VMEM((2, units_all, unit, width), BF16),
             pltpu.VMEM((3, units_all, unit, half), BF16),
             pltpu.VMEM((2, units_all, unit, half), F32),
+            pltpu.VMEM((2, units_all, unit, half), F32),
             pltpu.VMEM((2, units_all, unit, width), BF16),
             pltpu.VMEM((3, units_all, unit, half), BF16),
+            pltpu.VMEM((units_all, unit, width), BF16),
             pltpu.VMEM((2, width, half), BF16),
             pltpu.VMEM((2, width // 2, half - main), BF16),
-            pltpu.VMEM((2, 2, longest, chunk, main), BF16),
-            pltpu.VMEM((2, 2, longest, chunk, half), BF16),
+            pltpu.VMEM((2, 2, 2, longest, chunk, main), BF16),
+            pltpu.VMEM((2, 2, longest, chunk, half - main), BF16),
             pltpu.VMEM((2, chunk, main), BF16),
             pltpu.VMEM((2, 2, share, half), F32),
             pltpu.VMEM((2, share, half), F32),
@@ -765,17 +824,17 @@
             pltpu.VMEM((replicas, share, cols), F32),
             pltpu.VMEM((sections, final, cols), F32),
             pltpu.VMEM((final, cols), F32),
-            dma((3,)),
-            dma((units_all,)),
-            dma((units_all,)),
+            dma((4,)),
+            dma((units_all, 2)),
+            dma((units_all, 2)),
             dma((2,)),
             dma((2,)),
             dma((2, units_all)),
             dma((2, units_all)),
             dma((2,)),
             dma((2,)),
-            dma((2, 2, 2, longest)),
-            dma((2, 2, 2, longest)),
+            dma((3, 2, 2, longest)),
+            dma((3, 2, 2, longest)),
             dma((2,)),
             dma((2,)),
             dma((2,)),

time: 124 us -> 124 us (level)
  no operation moved by 1% of the time
where the time goes in v4:
time: 124 us
  Pallas kernels  124 us (100%)
    pallas_call x1, Pallas kernels, local(): pl.pallas_call(functools.partial(body, sections, replicas), out_shape=(ja...  121 us

profile of v4, /device:TPU:1, one launch (start us, length us, event | category | flops | bytes accessed | tf_op | source)
XLA Modules:
  0.0 124.2 jit_solution(7266239973293069722)
XLA Ops:
  0.6 121.4 %shard_map.129 = (bf16[8,32,1024]{2,1,0:T(8,128)(2,1)}, f32[32,2048]{1,0:T(8,128)}, f32[32,2048]{1,0:T(8,128)}, f32[4,128]{1,0:T(4,128)}) custom-call(s32[4]{0:T(128)} %plan_ref.1, s32[1,64]{1,0:T(1,128)} %bitcast.14, bf16[4,64,1024]{2,1,0:T(8,128)(2,1)} %bitcast.11, f32[1,1024]{1,0:T(1,128)} %gain_ref.1, bf16[1024,2048]{1,0:T(8,128)(2,1)} %bitcast.9, ...), custom_call_target="tpu_custom_call" | custom-call | tf_op jit(solution)/shard_map/pallas_call | solution.py:777
  122.1 2.1 %shard_map.130 = (bf16[8,32,1024]{2,1,0:T(8,128)(2,1)}, f32[32,2048]{1,0:T(8,128)}, f32[32,2048]{1,0:T(8,128)}, f32[4,128]{1,0:T(4,128)}) custom-call(bf16[8,32,1024]{2,1,0:T(8,128)(2,1)} %get-tuple-element.12.refs_0_, f32[32,2048]{1,0:T(8,128)} %get-tuple-element.13.refs_1_, f32[32,2048]{1,0:T(8,128)} %get-tuple-element.14.refs_2_, ...), custom_call_target="tpu_custom_call" | custom-call | tf_op jit(solution)/shard_map/pallas_call | solution.py:864

commit v5 on v4

--- a/solution.py
+++ b/solution.py
@@ -96,12 +96,11 @@
     slopes,
     hiddens,
     cots,
+    sided,
     backs,
     grads,
     products,
-    early,
-    ring_main,
-    ring_early,
+    ring,
     across,
     halves,
     mates,
@@ -120,8 +119,10 @@
     pair_recv,
     slot_send,
     slot_recv,
-    early_send,
-    early_recv,
+    far_send,
+    far_recv,
+    relay_send,
+    relay_recv,
     ring_send,
     ring_recv,
     across_send,
@@ -143,9 +144,8 @@
     levels = replicas // 4
     positions = replicas // 2
     chunk = width // (2 * levels)
-    side_rows = width // 2
-    main = ring_main.shape[-1]
     column_half = width // 2
+    quarter = half // 2
     share = width // replicas
     final = head_mine.shape[0]
 
@@ -157,6 +157,7 @@
     is_last = section == sections - 1
     not_last = section < sections - 1
     not_first = section > 0
+    streams = section < max(sections // 2 - 1, 1)
 
     def member(side_of, level_of, core_of):
         return (section, (side_of * levels + level_of) * 2 + core_of)
@@ -165,6 +166,7 @@
     behind = member(side, lax.rem(level + levels - 1, levels), core)
     mate = member(side, level, 1 - core)
     opposite = member(1 - side, level, core)
+    diagonal = member(1 - side, level, 1 - core)
     sender = (lax.rem(section + 1, sections), me)
     receiver = (lax.rem(section + sections - 1, sections), me)
     head_source = lax.div(section * replicas + me, sections)
@@ -195,7 +197,7 @@
     @pl.when(not_last)
     def _():
         greet(sender)
-        for device in (ahead, behind, mate, opposite):
+        for device in (ahead, behind, mate, opposite, diagonal):
             greet(device)
 
     @pl.when(is_last)
@@ -219,7 +221,7 @@
         values = values.astype(F32)
         inverse = inverse_rms(values)
         inverses[these] = inverse.reshape(per_slot, unit, 1)
-        normed[0, these] = (
+        normed[3, these] = (
             (values * inverse * gain_ref[...]).astype(BF16).reshape(per_slot, unit, width)
         )
         return unused
@@ -229,7 +231,7 @@
     heard = jnp.where(
         is_last,
         replicas + sections - jnp.where(me == replicas - 1, 1, 0),
-        4 + jnp.where(not_first, 1, 0),
+        5 + jnp.where(not_first, 1, 0),
     )
     pl.semaphore_wait(barrier, heard)
 
@@ -273,14 +275,19 @@
         lax.fori_loop(1, positions, send, 0)
         full_head[position, core] = head_ref[...]
 
-    normed_copy = remote(normed.at[0], normed.at[1], pair_send.at[0], pair_recv.at[0], mate)
+    normed_copy = remote(normed.at[3], normed.at[0], pair_send.at[0], pair_recv.at[0], mate)
     normed_copy.start()
+    normed_far = remote(normed.at[3], normed.at[1], pair_send.at[1], pair_recv.at[1], opposite)
+    normed_relay = remote(normed.at[1], normed.at[2], pair_send.at[2], pair_recv.at[2], mate)
+    active_copy = remote(active.at[4], active.at[0], pair_send.at[3], pair_recv.at[3], mate)
+    active_far = remote(active.at[3], active.at[1], pair_send.at[4], pair_recv.at[4], opposite)
+    active_cross = remote(active.at[4], active.at[2], pair_send.at[5], pair_recv.at[5], diagonal)
 
     down_load.wait()
     step = min(256, half)
-    all_normed = normed[0].reshape(rows_all, width)
+    all_normed = normed[3].reshape(rows_all, width)
     for part in range(2):
-        where = 2 * lax.rem(core + part, 2)
+        where = 3 + lax.rem(core + part, 2)
 
         def forward(number, unused, part=part, where=where):
             columns = pl.ds(pl.multiple_of(part * half + number * step, step), step)
@@ -297,7 +304,6 @@
 
         lax.fori_loop(0, half // step, forward, 0)
 
-    active_copy = remote(active.at[2], active.at[1], pair_send.at[1], pair_recv.at[1], mate)
     active_copy.start()
     up_load.wait()
 
@@ -309,7 +315,7 @@
             columns = pl.ds(pl.multiple_of(number * wide_step, wide_step), wide_step)
             total = wide[:, :, columns].astype(F32).reshape(rows_all, wide_step)
             for part in range(2):
-                where = 2 * lax.rem(core + part, 2)
+                where = 3 + lax.rem(core + part, 2)
                 total = total + matmul(
                     active[where].reshape(rows_all, half),
                     up[columns, part * half : (part + 1) * half],
@@ -338,6 +344,10 @@
         lax.fori_loop(1, positions, arrive, 0)
         gather_mate(core).start()
         gather_mate(1 - core).wait_recv()
+
+    normed_far.start()
+    active_far.start()
+    active_cross.start()
 
     def head_slot(slot):
         these = pl.ds(slot * per_slot, per_slot)
@@ -354,27 +364,58 @@
         head_slopes[these] = slope.reshape(per_slot, unit, slope.shape[1])
         upstream = matmul(slope, head, NT)
         cotangent = norm_backward(values, inverse, head_gain_ref[...], upstream)
-        cots[0, these] = cotangent.astype(BF16).reshape(per_slot, unit, width)
+        cots[these] = cotangent.astype(BF16).reshape(per_slot, unit, width)
 
     def cot_copy(slot, piece):
         columns = slice(piece * column_half, (piece + 1) * column_half)
         return remote(
             grads.at[slot, :, columns],
-            cots.at[0, slot, :, columns],
+            cots.at[slot, :, columns],
             cot_send.at[slot, piece],
             cot_recv.at[slot, piece],
             receiver,
         )
 
-    def pass_cot(slot):
-        return remote(
-            cots.at[0, slot], cots.at[1, slot], slot_send.at[0, slot], slot_recv.at[0, slot], mate
-        )
-
-    def pass_back(slot):
-        return remote(
-            backs.at[2, slot], backs.at[1, slot], slot_send.at[1, slot], slot_recv.at[1, slot], mate
-        )
+    def slot_copies(slot):
+        these = pl.ds(slot * per_slot, per_slot)
+        return (
+            remote(
+                sided.at[3, these], sided.at[0, these], slot_send.at[0, slot], slot_recv.at[0, slot], mate
+            ),
+            remote(
+                backs.at[4, these], backs.at[0, these], slot_send.at[1, slot], slot_recv.at[1, slot], mate
+            ),
+        )
+
+    def far_copies(number):
+        theirs = pl.ds(pl.multiple_of((1 - side) * column_half, column_half), column_half)
+        return (
+            remote(
+                backs.at[5, number], backs.at[1, number], far_send.at[0, number], far_recv.at[0, number], opposite
+            ),
+            remote(
+                backs.at[6, number], backs.at[2, number], far_send.at[1, number], far_recv.at[1, number], diagonal
+            ),
+            remote(
+                cots.at[number, :, theirs],
+                sided.at[1, number],
+                far_send.at[2, number],
+                far_recv.at[2, number],
+                opposite,
+            ),
+        )
+
+    def relay_copy(slot):
+        these = pl.ds(slot * per_slot, per_slot)
+        return remote(sided.at[1, these], sided.at[2, these], relay_send.at[slot], relay_recv.at[slot], mate)
+
+    def send_slot(slot):
+        for copy in slot_copies(slot):
+            copy.start()
+
+    def send_far(number):
+        for copy in far_copies(number):
+            copy.start()
 
     def backward(first, count, arriving):
         these = pl.ds(first, count)
@@ -384,14 +425,18 @@
             if arriving:
                 cot_copy(first, piece).wait_recv()
             columns = slice(piece * column_half, (piece + 1) * column_half)
-            part = matmul(cots[0, these, :, columns].reshape(rows, column_half), up[columns, :])
+            part = matmul(cots[these, :, columns].reshape(rows, column_half), up[columns, :])
             back_active = part if back_active is None else back_active + part
         dot = jnp.zeros((rows, 1), F32)
         back_parts = []
         for part in range(2):
             columns = slice(part * half, (part + 1) * half)
             back = (back_active[:, columns] * slopes[part, these].reshape(rows, half)).astype(BF16)
-            backs[2 * lax.rem(core + part, 2), these] = back.reshape(count, unit, half)
+            for of_side in range(2):
+                role = lax.rem(core + part, 2) + 2 * lax.rem(side + of_side, 2)
+                backs[3 + role, these] = back[:, of_side * quarter : (of_side + 1) * quarter].reshape(
+                    count, unit, quarter
+                )
             dot = dot + jnp.sum(
                 back.astype(F32) * hiddens[part, these].reshape(rows, half), axis=-1, keepdims=True
             )
@@ -404,7 +449,7 @@
                 back_parts[1], down_turned[half : 2 * half, columns]
             )
             grad = (
-                cots[0, these, :, columns].astype(F32).reshape(rows, column_half)
+                cots[these, :, columns].astype(F32).reshape(rows, column_half)
                 + inverse * (gain_ref[:, columns] * back_normed)
                 - wide[these, :, columns].astype(F32).reshape(rows, column_half) * pull
             )
@@ -415,15 +460,20 @@
                 for number in range(count):
                     cot_copy(first + number, piece).start()
 
-        for number in range(count):
-            pass_cot(first + number).start()
-            pass_back(first + number).start()
+        ours = pl.ds(pl.multiple_of(side * column_half, column_half), column_half)
+        sided[3, these] = cots[these, :, ours]
+
+        @pl.when(streams)
+        def _():
+            for number in range(count):
+                send_far(first + number)
 
     @pl.when(is_last)
     def _():
         def from_head(slot, unused):
             head_slot(slot)
             backward(slot * per_slot, per_slot, False)
+            send_slot(slot)
             return unused
 
         lax.fori_loop(0, micro, from_head, 0)
@@ -432,6 +482,11 @@
     def _():
         def from_next(number, unused):
             backward(number, 1, True)
+
+            @pl.when(lax.rem(number, per_slot) == per_slot - 1)
+            def _():
+                send_slot(lax.div(number, per_slot))
+
             return unused
 
         lax.fori_loop(0, units, from_next, 0)
@@ -439,123 +494,118 @@
     grads_copy = pltpu.make_async_copy(grads, grads_out, load_sem.at[3])
     grads_copy.start()
 
-    row_step = min(256, side_rows)
-
-    def multiply(matrix, of_side):
-        left, right = (normed, backs) if matrix == 0 else (cots, active)
-
+    @pl.when(jnp.logical_not(streams))
+    def _():
+        def send(number, unused):
+            send_far(number)
+            return unused
+
+        lax.fori_loop(0, units, send, 0)
+
+    row_step = min(256, column_half)
+    tokens_all = 4 * rows_all
+
+    def multiply(item):
         def block(number, unused):
-            first = of_side * side_rows + number * row_step
+            first = number * row_step
             rows = pl.ds(pl.multiple_of(first, row_step), row_step)
-            products[matrix, rows] = matmul(
-                left[:, :, :, rows].reshape(2 * rows_all, row_step),
-                right[0:2].reshape(2 * rows_all, half),
-                TN,
+            if item < 2:
+                of_side = 1 - side if item == 0 else side
+                columns = pl.ds(pl.multiple_of(of_side * column_half + first, row_step), row_step)
+                left, right = normed[:, :, :, columns], backs[0:4]
+            else:
+                left = sided[:, :, :, rows]
+                right = active[0:4, :, :, (item - 2) * quarter : (item - 1) * quarter]
+            products[item, rows] = matmul(
+                left.reshape(tokens_all, row_step), right.reshape(tokens_all, quarter), TN
             ).astype(BF16)
             return unused
 
-        lax.fori_loop(0, side_rows // row_step, block, 0)
-
-    theirs_rows = pl.ds(pl.multiple_of((1 - side) * side_rows, side_rows), side_rows)
-
-    def early_copy(matrix):
+        lax.fori_loop(0, column_half // row_step, block, 0)
+
+    longest = levels // 2
+
+    def hops(item, way):
+        return longest if item % 2 == way else longest - 1
+
+    def rows_of(position):
+        return pl.ds(pl.multiple_of(position * chunk, chunk), chunk)
+
+    def ring_rows(item, way, hop):
+        left = hops(item, way) - hop
+        return rows_of(lax.rem(level + levels + (left if way == 0 else -left), levels))
+
+    def ring_copy(item, way, hop):
         return remote(
-            products.at[matrix, theirs_rows, main:half],
-            early.at[matrix],
-            early_send.at[matrix],
-            early_recv.at[matrix],
-            opposite,
-        )
-
-    longest = levels // 2
-    phase_columns = (slice(0, main), slice(0, main), slice(main, half))
-
-    def buffer_of(phase):
-        return ring_early if phase == 2 else ring_main.at[phase]
-
-    def hops(matrix, way):
-        return longest if matrix == way else longest - 1
-
-    def rows_of(phase, position):
-        side_of = 1 - side if phase == 0 else side
-        return pl.ds(pl.multiple_of((side_of * levels + position) * chunk, chunk), chunk)
-
-    def ring_rows(phase, matrix, way, hop):
-        left = hops(matrix, way) - hop
-        return rows_of(phase, lax.rem(level + levels + (left if way == 0 else -left), levels))
-
-    def ring_copy(phase, matrix, way, hop):
-        return remote(
-            products.at[matrix, ring_rows(phase, matrix, way, hop), phase_columns[phase]],
-            buffer_of(phase).at[matrix, way, hop],
-            ring_send.at[phase, matrix, way, hop],
-            ring_recv.at[phase, matrix, way, hop],
+            products.at[item, ring_rows(item, way, hop)],
+            ring.at[item, way, hop],
+            ring_send.at[item, way, hop],
+            ring_recv.at[item, way, hop],
             ahead if way == 0 else behind,
         )
 
-    def ways_of(matrix):
-        return (0, 1) if matrix == 0 else (1, 0)
-
-    def ring_start(phase, matrix):
-        for way in ways_of(matrix):
-            ring_copy(phase, matrix, way, 0).start()
-
-    def ring_turn(phase, matrix, hop):
-        columns = phase_columns[phase]
-        for way in ways_of(matrix):
-            if 0 < hop < hops(matrix, way):
-                ring_copy(phase, matrix, way, hop - 1).wait_recv()
-                rows = ring_rows(phase, matrix, way, hop)
-                total = products[matrix, rows, columns].astype(F32) + (
-                    buffer_of(phase)[matrix, way, hop - 1].astype(F32)
-                )
-                products[matrix, rows, columns] = total.astype(BF16)
-                ring_copy(phase, matrix, way, hop).start()
-
-    def ring_total(phase, matrix):
-        total = products[matrix, rows_of(phase, level), phase_columns[phase]].astype(F32)
-        for way in reversed(ways_of(matrix)):
-            last = hops(matrix, way) - 1
-            ring_copy(phase, matrix, way, last).wait_recv()
-            total = total + buffer_of(phase)[matrix, way, last].astype(F32)
+    def ways_of(item):
+        return (0, 1) if item % 2 == 0 else (1, 0)
+
+    def ring_start(item):
+        for way in ways_of(item):
+            ring_copy(item, way, 0).start()
+
+    def ring_turn(item, hop):
+        for way in ways_of(item):
+            if hop < hops(item, way):
+                ring_copy(item, way, hop - 1).wait_recv()
+                rows = ring_rows(item, way, hop)
+                total = products[item, rows].astype(F32) + ring[item, way, hop - 1].astype(F32)
+                products[item, rows] = total.astype(BF16)
+                ring_copy(item, way, hop).start()
+
+    def ring_total(item):
+        total = products[item, rows_of(level)].astype(F32)
+        for way in reversed(ways_of(item)):
+            last = hops(item, way) - 1
+            ring_copy(item, way, last).wait_recv()
+            total = total + ring[item, way, last].astype(F32)
         return total
 
-    def add_early(matrix):
-        early_copy(matrix).wait_recv()
-
-        def add(number, unused):
-            rows = pl.ds(pl.multiple_of(side * side_rows + number * chunk, chunk), chunk)
-            from_rows = pl.ds(pl.multiple_of(number * chunk, chunk), chunk)
-            total = products[matrix, rows, main:half].astype(F32) + (
-                early[matrix, from_rows].astype(F32)
-            )
-            products[matrix, rows, main:half] = total.astype(BF16)
-            return unused
-
-        lax.fori_loop(0, levels, add, 0)
-
-    def cot_passed(number, unused):
-        pass_cot(number).wait_recv()
+    normed_far.wait_recv()
+    normed_relay.start()
+
+    def relay_slot(slot, unused):
+        for number in range(per_slot):
+            far_copies(slot * per_slot + number)[2].wait_recv()
+        relay_copy(slot).start()
         return unused
 
-    def back_passed(number, unused):
-        pass_back(number).wait_recv()
+    lax.fori_loop(0, micro, relay_slot, 0)
+
+    def backs_arrived(slot, unused):
+        slot_copies(slot)[1].wait_recv()
+        for number in range(per_slot):
+            for copy in far_copies(slot * per_slot + number)[:2]:
+                copy.wait_recv()
         return unused
 
+    lax.fori_loop(0, micro, backs_arrived, 0)
     normed_copy.wait_recv()
-    active_copy.wait_recv()
-    lax.fori_loop(0, units, cot_passed, 0)
-    multiply(1, 1 - side)
-    early_copy(1).start()
-    ring_start(0, 1)
-    lax.fori_loop(0, units, back_passed, 0)
-    multiply(0, 1 - side)
-    early_copy(0).start()
-    ring_start(0, 0)
-    multiply(1, side)
-    ring_start(1, 1)
-    multiply(0, side)
-    ring_start(1, 0)
+    normed_relay.wait_recv()
+    multiply(0)
+    ring_start(0)
+    multiply(1)
+    ring_start(1)
+
+    def cots_arrived(slot, unused):
+        slot_copies(slot)[0].wait_recv()
+        relay_copy(slot).wait_recv()
+        return unused
+
+    lax.fori_loop(0, micro, cots_arrived, 0)
+    for copy in (active_copy, active_far, active_cross):
+        copy.wait_recv()
+    multiply(2)
+    ring_start(2)
+    multiply(3)
+    ring_start(3)
 
     def term_copy(offset):
         peer = lax.rem(me + offset, replicas)
@@ -589,41 +639,14 @@
 
         lax.fori_loop(1, replicas, send, 0)
 
-    def across_copy(matrix):
-        return remote(
-            products.at[matrix, rows_of(0, level), 0:main],
-            across.at[matrix],
-            across_send.at[matrix],
-            across_recv.at[matrix],
-            opposite,
-        )
-
+    across_copy = remote(
+        products.at[0, rows_of(level)], across, across_send.at[0], across_recv.at[0], opposite
+    )
     for hop in range(1, longest):
-        for phase in (0, 1):
-            for matrix in (1, 0):
-                ring_turn(phase, matrix, hop)
-        if hop == 1:
-            add_early(1)
-            ring_start(2, 1)
-        elif hop == 2:
-            add_early(0)
-            ring_start(2, 0)
-            ring_turn(2, 1, 1)
-        elif hop == 3:
-            ring_turn(2, 0, 1)
-            ring_turn(2, 1, 2)
-    if longest < 3:
-        add_early(0)
-        ring_start(2, 0)
-        ring_turn(2, 1, 1)
-        ring_turn(2, 0, 1)
-    for matrix in (1, 0):
-        products[matrix, rows_of(0, level), 0:main] = ring_total(0, matrix).astype(BF16)
-        across_copy(matrix).start()
-    if longest >= 3:
-        ring_turn(2, 0, 2)
-        ring_turn(2, 1, 3)
-        ring_turn(2, 0, 3)
+        for item in range(4):
+            ring_turn(item, hop)
+    products[0, rows_of(level)] = ring_total(0).astype(BF16)
+    across_copy.start()
 
     def mate_copy(matrix):
         return remote(
@@ -632,16 +655,21 @@
 
     mine = pl.ds(pl.multiple_of(core * half, half), half)
     theirs = pl.ds(pl.multiple_of((1 - core) * half, half), half)
-    for matrix in (1, 0):
-        total = ring_total(1, matrix)
-        across_copy(matrix).wait_recv()
-        total = (total + across[matrix].astype(F32)) / LOSS_SCALE
-        halves[matrix, :, :, 0:main] = total.reshape(2, share, main)
-    for matrix, result in ((1, up_out), (0, down_out)):
-        total = ring_total(2, matrix) / LOSS_SCALE
-        halves[matrix, :, :, main:half] = total.reshape(2, share, half - main)
-        mate_copy(matrix).start()
-        result[:, mine] = halves[matrix, core]
+    halves[0, :, :, pl.ds(pl.multiple_of(side * quarter, quarter), quarter)] = (
+        ring_total(1) / LOSS_SCALE
+    ).reshape(2, share, quarter)
+    for item in (2, 3):
+        halves[1, :, :, (item - 2) * quarter : (item - 1) * quarter] = (
+            ring_total(item) / LOSS_SCALE
+        ).reshape(2, share, quarter)
+    mate_copy(1).start()
+    up_out[:, mine] = halves[1, core]
+    across_copy.wait_recv()
+    halves[0, :, :, pl.ds(pl.multiple_of((1 - side) * quarter, quarter), quarter)] = (
+        across[...].astype(F32) / LOSS_SCALE
+    ).reshape(2, share, quarter)
+    mate_copy(0).start()
+    down_out[:, mine] = halves[0, core]
 
     @pl.when(is_last)
     def _():
@@ -664,7 +692,7 @@
             def _():
                 copy.start()
 
-    for matrix, result in ((0, down_out), (1, up_out)):
+    for matrix, result in ((1, up_out), (0, down_out)):
         mate_copy(matrix).wait_recv()
         result[:, theirs] = mates[matrix]
 
@@ -675,15 +703,27 @@
     head_out[...] = head_mine[...]
 
     grads_copy.wait()
-    normed_copy.wait_send()
-    active_copy.wait_send()
+    for copy in (
+        normed_copy,
+        normed_far,
+        normed_relay,
+        active_copy,
+        active_far,
+        active_cross,
+        across_copy,
+    ):
+        copy.wait_send()
 
     def slot_left(slot, unused):
-        pass_cot(slot).wait_send()
-        pass_back(slot).wait_send()
+        for copy in slot_copies(slot):
+            copy.wait_send()
+        relay_copy(slot).wait_send()
+        for number in range(per_slot):
+            for copy in far_copies(slot * per_slot + number):
+                copy.wait_send()
         return unused
 
-    lax.fori_loop(0, units, slot_left, 0)
+    lax.fori_loop(0, micro, slot_left, 0)
 
     @pl.when(not_first)
     def _():
@@ -694,14 +734,11 @@
 
         lax.fori_loop(0, units, cot_left, 0)
 
-    for phase in range(3):
-        for matrix in range(2):
-            for way in range(2):
-                for hop in range(hops(matrix, way)):
-                    ring_copy(phase, matrix, way, hop).wait_send()
+    for item in range(4):
+        for way in range(2):
+            for hop in range(hops(item, way)):
+                ring_copy(item, way, hop).wait_send()
     for matrix in range(2):
-        early_copy(matrix).wait_send()
-        across_copy(matrix).wait_send()
         mate_copy(matrix).wait_send()
 
     @pl.when(is_last)
@@ -769,7 +806,7 @@
     final = share // sections
     unit = tokens // 2
     units_all = 2 * micro
-    main = half - half // 4
+    quarter = half // 2
     longest = rings // 2
     whole = pl.BlockSpec(memory_space=pltpu.VMEM)
     anywhere = pl.BlockSpec(memory_space=pl.ANY)
@@ -802,18 +839,17 @@
             pltpu.VMEM((units, width), BF16),
             pltpu.VMEM((units_all, unit, width), BF16),
             pltpu.VMEM((units_all, unit, 1), F32),
-            pltpu.VMEM((2, units_all, unit, width), BF16),
-            pltpu.VMEM((3, units_all, unit, half), BF16),
+            pltpu.VMEM((4, units_all, unit, width), BF16),
+            pltpu.VMEM((5, units_all, unit, half), BF16),
             pltpu.VMEM((2, units_all, unit, half), F32),
             pltpu.VMEM((2, units_all, unit, half), F32),
-            pltpu.VMEM((2, units_all, unit, width), BF16),
-            pltpu.VMEM((3, units_all, unit, half), BF16),
             pltpu.VMEM((units_all, unit, width), BF16),
-            pltpu.VMEM((2, width, half), BF16),
-            pltpu.VMEM((2, width // 2, half - main), BF16),
-            pltpu.VMEM((2, 2, 2, longest, chunk, main), BF16),
-            pltpu.VMEM((2, 2, longest, chunk, half - main), BF16),
-            pltpu.VMEM((2, chunk, main), BF16),
+            pltpu.VMEM((4, units_all, unit, width // 2), BF16),
+            pltpu.VMEM((7, units_all, unit, quarter), BF16),
+            pltpu.VMEM((units_all, unit, width), BF16),
+            pltpu.VMEM((4, width // 2, quarter), BF16),
+            pltpu.VMEM((4, 2, longest, chunk, quarter), BF16),
+            pltpu.VMEM((chunk, quarter), BF16),
             pltpu.VMEM((2, 2, share, half), F32),
             pltpu.VMEM((2, share, half), F32),
             pltpu.VMEM((replicas // 2, 2, share, cols), BF16),
@@ -827,16 +863,18 @@
             dma((4,)),
             dma((units_all, 2)),
             dma((units_all, 2)),
-            dma((2,)),
-            dma((2,)),
-            dma((2, units_all)),
-            dma((2, units_all)),
-            dma((2,)),
-            dma((2,)),
-            dma((3, 2, 2, longest)),
-            dma((3, 2, 2, longest)),
-            dma((2,)),
-            dma((2,)),
+            dma((6,)),
+            dma((6,)),
+            dma((2, micro)),
+            dma((2, micro)),
+            dma((3, units_all)),
+            dma((3, units_all)),
+            dma((micro,)),
+            dma((micro,)),
+            dma((4, 2, longest)),
+            dma((4, 2, longest)),
+            dma((1,)),
+            dma((1,)),
             dma((2,)),
             dma((2,)),
             dma((replicas // 2,)),

time: 124 us -> 133 us (1.073)
  Pallas kernels: 124 us -> 133 us
    pallas_call x1, Pallas kernels: 121 us -> 130 us  [local(): pl.pallas_call(functools.partial(body, sections, replicas), out_shape=(ja...]
where the time goes in v5:
time: 133 us
  Pallas kernels  133 us (100%)
    pallas_call x1, Pallas kernels, local(): pl.pallas_call(functools.partial(body, sections, replicas), out_shape=(ja...  130 us

profile of v5, /device:TPU:1, one launch (start us, length us, event | category | flops | bytes accessed | tf_op | source)
XLA Modules:
  0.0 133.2 jit_solution(11851793863405044971)
XLA Ops:
  0.6 130.5 %shard_map.129 = (bf16[8,32,1024]{2,1,0:T(8,128)(2,1)}, f32[32,2048]{1,0:T(8,128)}, f32[32,2048]{1,0:T(8,128)}, f32[4,128]{1,0:T(4,128)}) custom-call(s32[4]{0:T(128)} %plan_ref.1, s32[1,64]{1,0:T(1,128)} %bitcast.14, bf16[4,64,1024]{2,1,0:T(8,128)(2,1)} %bitcast.11, f32[1,1024]{1,0:T(1,128)} %gain_ref.1, bf16[1024,2048]{1,0:T(8,128)(2,1)} %bitcast.9, ...), custom_call_target="tpu_custom_call" | custom-call | tf_op jit(solution)/shard_map/pallas_call | solution.py:814
  131.1 2.1 %shard_map.130 = (bf16[8,32,1024]{2,1,0:T(8,128)(2,1)}, f32[32,2048]{1,0:T(8,128)}, f32[32,2048]{1,0:T(8,128)}, f32[4,128]{1,0:T(4,128)}) custom-call(bf16[8,32,1024]{2,1,0:T(8,128)(2,1)} %get-tuple-element.12.refs_0_, f32[32,2048]{1,0:T(8,128)} %get-tuple-element.13.refs_1_, f32[32,2048]{1,0:T(8,128)} %get-tuple-element.14.refs_2_, ...), custom_call_target="tpu_custom_call" | custom-call | tf_op jit(solution)/shard_map/pallas_call | solution.py:902

commit v6 on v5

--- a/solution.py
+++ b/solution.py
@@ -283,6 +283,7 @@
     active_far = remote(active.at[3], active.at[1], pair_send.at[4], pair_recv.at[4], opposite)
     active_cross = remote(active.at[4], active.at[2], pair_send.at[5], pair_recv.at[5], diagonal)
 
+    normed_far.start()
     down_load.wait()
     step = min(256, half)
     all_normed = normed[3].reshape(rows_all, width)
@@ -305,6 +306,8 @@
         lax.fori_loop(0, half // step, forward, 0)
 
     active_copy.start()
+    active_far.start()
+    active_cross.start()
     up_load.wait()
 
     @pl.when(is_last)
@@ -344,10 +347,6 @@
         lax.fori_loop(1, positions, arrive, 0)
         gather_mate(core).start()
         gather_mate(1 - core).wait_recv()
-
-    normed_far.start()
-    active_far.start()
-    active_cross.start()
 
     def head_slot(slot):
         these = pl.ds(slot * per_slot, per_slot)
@@ -494,6 +493,38 @@
     grads_copy = pltpu.make_async_copy(grads, grads_out, load_sem.at[3])
     grads_copy.start()
 
+    def term_copy(offset):
+        peer = lax.rem(me + offset, replicas)
+        return remote(
+            head_parts.at[peer], head_terms.at[me], term_send.at[offset], term_recv.at[me], (section, peer)
+        )
+
+    def term_wait(offset):
+        peer = lax.rem(me + offset, replicas)
+        remote(
+            head_parts.at[peer], head_terms.at[peer], term_send.at[offset], term_recv.at[peer], (section, peer)
+        ).wait_recv()
+
+    def share_copy(number):
+        block = sections * me + number
+        target = (lax.div(block, replicas), lax.rem(block, replicas))
+        return block, remote(head_sums.at[number], head_mine, share_send.at[number], share_recv, target)
+
+    @pl.when(is_last)
+    def _():
+        part = matmul(
+            head_ins[...].reshape(rows_all, width),
+            head_slopes[...].reshape(rows_all, head_slopes.shape[2]),
+            TN,
+        )
+        head_parts[...] = part.reshape(head_parts.shape)
+
+        def send(offset, unused):
+            term_copy(offset).start()
+            return unused
+
+        lax.fori_loop(1, replicas, send, 0)
+
     @pl.when(jnp.logical_not(streams))
     def _():
         def send(number, unused):
@@ -607,37 +638,26 @@
     multiply(3)
     ring_start(3)
 
-    def term_copy(offset):
-        peer = lax.rem(me + offset, replicas)
-        return remote(
-            head_parts.at[peer], head_terms.at[me], term_send.at[offset], term_recv.at[me], (section, peer)
-        )
-
-    def term_wait(offset):
-        peer = lax.rem(me + offset, replicas)
-        remote(
-            head_parts.at[peer], head_terms.at[peer], term_send.at[offset], term_recv.at[peer], (section, peer)
-        ).wait_recv()
-
-    def share_copy(number):
-        block = sections * me + number
-        target = (lax.div(block, replicas), lax.rem(block, replicas))
-        return block, remote(head_sums.at[number], head_mine, share_send.at[number], share_recv, target)
-
     @pl.when(is_last)
     def _():
-        part = matmul(
-            head_ins[...].reshape(rows_all, width),
-            head_slopes[...].reshape(rows_all, head_slopes.shape[2]),
-            TN,
-        )
-        head_parts[...] = part.reshape(head_parts.shape)
-
-        def send(offset, unused):
-            term_copy(offset).start()
-            return unused
-
-        lax.fori_loop(1, replicas, send, 0)
+        def add_term(offset, total):
+            term_wait(offset)
+            return total + head_terms[lax.rem(me + offset, replicas)]
+
+        total = lax.fori_loop(1, replicas, add_term, head_parts[me]) / LOSS_SCALE
+        for number in range(sections):
+            head_sums[number] = total[number * final : (number + 1) * final]
+        for number in range(sections):
+            block, copy = share_copy(number)
+            to_me = block == (sections - 1) * replicas + me
+
+            @pl.when(to_me)
+            def _():
+                head_mine[...] = head_sums[number]
+
+            @pl.when(jnp.logical_not(to_me))
+            def _():
+                copy.start()
 
     across_copy = remote(
         products.at[0, rows_of(level)], across, across_send.at[0], across_recv.at[0], opposite
@@ -670,27 +690,6 @@
     ).reshape(2, share, quarter)
     mate_copy(0).start()
     down_out[:, mine] = halves[0, core]
-
-    @pl.when(is_last)
-    def _():
-        def add_term(offset, total):
-            term_wait(offset)
-            return total + head_terms[lax.rem(me + offset, replicas)]
-
-        total = lax.fori_loop(1, replicas, add_term, head_parts[me]) / LOSS_SCALE
-        for number in range(sections):
-            head_sums[number] = total[number * final : (number + 1) * final]
-        for number in range(sections):
-            block, copy = share_copy(number)
-            to_me = block == (sections - 1) * replicas + me
-
-            @pl.when(to_me)
-            def _():
-                head_mine[...] = head_sums[number]
-
-            @pl.when(jnp.logical_not(to_me))
-            def _():
-                copy.start()
 
     for matrix, result in ((1, up_out), (0, down_out)):
         mate_copy(matrix).wait_recv()

time: 133 us -> 116 us (0.87); the launches traced: 133 us -> 114 us
  Pallas kernels: 133 us -> 113 us
    pallas_call x1, Pallas kernels: 130 us -> 111 us  [local(): pl.pallas_call(functools.partial(body, sections, replicas), out_shape=(ja...]
where the time goes in v6:
time: 116 us; the launch traced here: 114 us
  Pallas kernels  113 us (97%)
    pallas_call x1, Pallas kernels, local(): pl.pallas_call(functools.partial(body, sections, replicas), out_shape=(ja...  111 us

profile of v6, /device:TPU:1, one launch (start us, length us, event | category | flops | bytes accessed | tf_op | source)
XLA Modules:
  0.0 113.8 jit_solution(6565905332967600347)
XLA Ops:
  0.6 111.1 %shard_map.129 = (bf16[8,32,1024]{2,1,0:T(8,128)(2,1)}, f32[32,2048]{1,0:T(8,128)}, f32[32,2048]{1,0:T(8,128)}, f32[4,128]{1,0:T(4,128)}) custom-call(s32[4]{0:T(128)} %plan_ref.1, s32[1,64]{1,0:T(1,128)} %bitcast.14, bf16[4,64,1024]{2,1,0:T(8,128)(2,1)} %bitcast.11, f32[1,1024]{1,0:T(1,128)} %gain_ref.1, bf16[1024,2048]{1,0:T(8,128)(2,1)} %bitcast.9, ...), custom_call_target="tpu_custom_call" | custom-call | tf_op jit(solution)/shard_map/pallas_call | solution.py:813
  111.8 2.1 %shard_map.130 = (bf16[8,32,1024]{2,1,0:T(8,128)(2,1)}, f32[32,2048]{1,0:T(8,128)}, f32[32,2048]{1,0:T(8,128)}, f32[4,128]{1,0:T(4,128)}) custom-call(bf16[8,32,1024]{2,1,0:T(8,128)(2,1)} %get-tuple-element.12.refs_0_, f32[32,2048]{1,0:T(8,128)} %get-tuple-element.13.refs_1_, f32[32,2048]{1,0:T(8,128)} %get-tuple-element.14.refs_2_, ...), custom_call_target="tpu_custom_call" | custom-call | tf_op jit(solution)/shard_map/pallas_call | solution.py:901

commit v7 on v6

--- a/solution.py
+++ b/solution.py
@@ -109,6 +109,8 @@
     head_ins,
     head_slopes,
     head_parts,
+    head_other,
+    head_added,
     head_terms,
     head_sums,
     head_mine,
@@ -135,6 +137,9 @@
     term_recv,
     share_send,
     share_recv,
+    other_send,
+    other_recv,
+    ready,
 ):
     units, unit, width = wide.shape
     micro = saved.shape[0]
@@ -200,17 +205,23 @@
         for device in (ahead, behind, mate, opposite, diagonal):
             greet(device)
 
+    position = side * levels + level
+
     @pl.when(is_last)
     def _():
         def greet_peer(offset, unused):
-            greet((section, lax.rem(me + offset, replicas)))
-            return unused
-
-        lax.fori_loop(1, replicas, greet_peer, 0)
-
-    @pl.when(jnp.logical_not(source_is_me))
-    def _():
-        greet((sections - 1, head_source))
+            greet((section, lax.rem(position + offset, positions) * 2 + core))
+            return unused
+
+        lax.fori_loop(1, positions, greet_peer, 0)
+        greet(mate)
+        greet(diagonal)
+        for number in range(sections):
+            block = sections * me + number
+
+            @pl.when(block != (sections - 1) * replicas + me)
+            def _():
+                greet((lax.div(block, replicas), lax.rem(block, replicas)))
 
     saved_load.wait()
 
@@ -230,12 +241,16 @@
 
     heard = jnp.where(
         is_last,
-        replicas + sections - jnp.where(me == replicas - 1, 1, 0),
-        5 + jnp.where(not_first, 1, 0),
+        positions + 3 - jnp.where(me == replicas - 1, 1, 0),
+        6 + jnp.where(not_first, 1, 0),
     )
     pl.semaphore_wait(barrier, heard)
 
-    position = side * levels + level
+    @pl.when(jnp.logical_not(source_is_me))
+    def _():
+        pl.semaphore_signal(
+            ready, inc=1, device_id=(sections - 1, head_source), device_id_type=MESH
+        )
 
     def gather_copy(offset):
         peer = lax.rem(position + offset, positions)
@@ -416,7 +431,7 @@
         for copy in far_copies(number):
             copy.start()
 
-    def backward(first, count, arriving):
+    def backward(first, count, arriving, passing, far):
         these = pl.ds(first, count)
         rows = count * unit
         back_active = None
@@ -454,33 +469,33 @@
             )
             grads[these, :, columns] = grad.astype(BF16).reshape(count, unit, column_half)
 
-            @pl.when(not_first)
+            if passing:
+                for number in range(count):
+                    cot_copy(first + number, piece).start()
+
+        ours = pl.ds(pl.multiple_of(side * column_half, column_half), column_half)
+        sided[3, these] = cots[these, :, ours]
+
+        if far:
+
+            @pl.when(streams)
             def _():
                 for number in range(count):
-                    cot_copy(first + number, piece).start()
-
-        ours = pl.ds(pl.multiple_of(side * column_half, column_half), column_half)
-        sided[3, these] = cots[these, :, ours]
-
-        @pl.when(streams)
-        def _():
-            for number in range(count):
-                send_far(first + number)
+                    send_far(first + number)
 
     @pl.when(is_last)
     def _():
         def from_head(slot, unused):
             head_slot(slot)
-            backward(slot * per_slot, per_slot, False)
+            backward(slot * per_slot, per_slot, False, True, False)
             send_slot(slot)
             return unused
 
         lax.fori_loop(0, micro, from_head, 0)
 
-    @pl.when(not_last)
-    def _():
+    def receive(passing):
         def from_next(number, unused):
-            backward(number, 1, True)
+            backward(number, 1, True, passing, True)
 
             @pl.when(lax.rem(number, per_slot) == per_slot - 1)
             def _():
@@ -490,19 +505,39 @@
 
         lax.fori_loop(0, units, from_next, 0)
 
+    @pl.when(jnp.logical_and(not_first, not_last))
+    def _():
+        receive(True)
+
+    @pl.when(jnp.logical_not(not_first))
+    def _():
+        receive(False)
+
     grads_copy = pltpu.make_async_copy(grads, grads_out, load_sem.at[3])
     grads_copy.start()
 
+    other_copy = remote(
+        head_parts.at[:, 1 - core], head_other, other_send, other_recv, mate
+    )
+
     def term_copy(offset):
-        peer = lax.rem(me + offset, replicas)
+        peer = lax.rem(position + offset, positions)
         return remote(
-            head_parts.at[peer], head_terms.at[me], term_send.at[offset], term_recv.at[me], (section, peer)
+            head_added.at[peer],
+            head_terms.at[position],
+            term_send.at[offset],
+            term_recv.at[position],
+            (section, peer * 2 + core),
         )
 
     def term_wait(offset):
-        peer = lax.rem(me + offset, replicas)
+        peer = lax.rem(position + offset, positions)
         remote(
-            head_parts.at[peer], head_terms.at[peer], term_send.at[offset], term_recv.at[peer], (section, peer)
+            head_added.at[peer],
+            head_terms.at[peer],
+            term_send.at[offset],
+            term_recv.at[peer],
+            (section, peer * 2 + core),
         ).wait_recv()
 
     def share_copy(number):
@@ -518,12 +553,15 @@
             TN,
         )
         head_parts[...] = part.reshape(head_parts.shape)
+        other_copy.start()
+        other_copy.wait_recv()
+        head_added[...] = head_parts[:, core] + head_other[...]
 
         def send(offset, unused):
             term_copy(offset).start()
             return unused
 
-        lax.fori_loop(1, replicas, send, 0)
+        lax.fori_loop(1, positions, send, 0)
 
     @pl.when(jnp.logical_not(streams))
     def _():
@@ -642,9 +680,10 @@
     def _():
         def add_term(offset, total):
             term_wait(offset)
-            return total + head_terms[lax.rem(me + offset, replicas)]
-
-        total = lax.fori_loop(1, replicas, add_term, head_parts[me]) / LOSS_SCALE
+            return total + head_terms[lax.rem(position + offset, positions)]
+
+        total = lax.fori_loop(1, positions, add_term, head_added[position]) / LOSS_SCALE
+        pl.semaphore_wait(ready, sections - jnp.where(me == replicas - 1, 1, 0))
         for number in range(sections):
             head_sums[number] = total[number * final : (number + 1) * final]
         for number in range(sections):
@@ -662,11 +701,19 @@
     across_copy = remote(
         products.at[0, rows_of(level)], across, across_send.at[0], across_recv.at[0], opposite
     )
-    for hop in range(1, longest):
-        for item in range(4):
-            ring_turn(item, hop)
-    products[0, rows_of(level)] = ring_total(0).astype(BF16)
-    across_copy.start()
+    turns = (
+        ((0, 1), (1, 1), (2, 1), (0, 2), (3, 1), (1, 2), (0, 3), (2, 2), (3, 2), (1, 3), (2, 3), (3, 3))
+        if longest == 4
+        else tuple((item, hop) for hop in range(1, longest) for item in range(4))
+    )
+    for number, (item, hop) in enumerate(turns):
+        ring_turn(item, hop)
+        if number == len(turns) - 2:
+            products[0, rows_of(level)] = ring_total(0).astype(BF16)
+            across_copy.start()
+    if not turns:
+        products[0, rows_of(level)] = ring_total(0).astype(BF16)
+        across_copy.start()
 
     def mate_copy(matrix):
         return remote(
@@ -744,15 +791,11 @@
     def _():
         def head_left(offset, unused):
             term_copy(offset).wait_send()
-            return unused
-
-        lax.fori_loop(1, replicas, head_left, 0)
-
-        def gather_left(offset, unused):
             gather_copy(offset).wait_send()
             return unused
 
-        lax.fori_loop(1, positions, gather_left, 0)
+        lax.fori_loop(1, positions, head_left, 0)
+        other_copy.wait_send()
         gather_mate(core).wait_send()
         for number in range(sections):
             block, copy = share_copy(number)
@@ -855,8 +898,10 @@
             pltpu.VMEM((units_all, unit, width), BF16),
             pltpu.VMEM((units_all, unit, width), BF16),
             pltpu.VMEM((units_all, unit, cols), BF16),
-            pltpu.VMEM((replicas, share, cols), F32),
-            pltpu.VMEM((replicas, share, cols), F32),
+            pltpu.VMEM((replicas // 2, 2, share, cols), F32),
+            pltpu.VMEM((replicas // 2, share, cols), F32),
+            pltpu.VMEM((replicas // 2, share, cols), F32),
+            pltpu.VMEM((replicas // 2, share, cols), F32),
             pltpu.VMEM((sections, final, cols), F32),
             pltpu.VMEM((final, cols), F32),
             dma((4,)),
@@ -878,10 +923,13 @@
             dma((2,)),
             dma((replicas // 2,)),
             dma((replicas // 2 + 1,)),
-            dma((replicas,)),
-            dma((replicas,)),
+            dma((replicas // 2,)),
+            dma((replicas // 2,)),
             dma((sections,)),
             dma(()),
+            dma(()),
+            dma(()),
+            pltpu.SemaphoreType.REGULAR,
         ],
         compiler_params=pltpu.CompilerParams(
             collective_id=0, has_side_effects=True, vmem_limit_bytes=56 * 1024 * 1024

time: 116 us -> 111 us (0.957)
  Pallas kernels: 113 us -> 109 us
    pallas_call x1, Pallas kernels: 111 us -> 107 us  [local(): pl.pallas_call(functools.partial(body, sections, replicas), out_shape=(ja...]
where the time goes in v7:
time: 111 us; the launch traced here: 110 us
  Pallas kernels  109 us (98%)
    pallas_call x1, Pallas kernels, local(): pl.pallas_call(functools.partial(body, sections, replicas), out_shape=(ja...  107 us

profile of v7, /device:TPU:1, one launch (start us, length us, event | category | flops | bytes accessed | tf_op | source)
XLA Modules:
  0.0 109.6 jit_solution(4905179607760640774)
XLA Ops:
  0.6 106.9 %shard_map.129 = (bf16[8,32,1024]{2,1,0:T(8,128)(2,1)}, f32[32,2048]{1,0:T(8,128)}, f32[32,2048]{1,0:T(8,128)}, f32[4,128]{1,0:T(4,128)}) custom-call(s32[4]{0:T(128)} %plan_ref.1, s32[1,64]{1,0:T(1,128)} %bitcast.14, bf16[4,64,1024]{2,1,0:T(8,128)(2,1)} %bitcast.11, f32[1,1024]{1,0:T(1,128)} %gain_ref.1, bf16[1024,2048]{1,0:T(8,128)(2,1)} %bitcast.9, ...), custom_call_target="tpu_custom_call" | custom-call | tf_op jit(solution)/shard_map/pallas_call | solution.py:856
  107.5 2.1 %shard_map.130 = (bf16[8,32,1024]{2,1,0:T(8,128)(2,1)}, f32[32,2048]{1,0:T(8,128)}, f32[32,2048]{1,0:T(8,128)}, f32[4,128]{1,0:T(4,128)}) custom-call(bf16[8,32,1024]{2,1,0:T(8,128)(2,1)} %get-tuple-element.12.refs_0_, f32[32,2048]{1,0:T(8,128)} %get-tuple-element.13.refs_1_, f32[32,2048]{1,0:T(8,128)} %get-tuple-element.14.refs_2_, ...), custom_call_target="tpu_custom_call" | custom-call | tf_op jit(solution)/shard_map/pallas_call | solution.py:949

commit v8 on v7

--- a/solution.py
+++ b/solution.py
@@ -71,20 +71,27 @@
 def body(
     sections,
     replicas,
+    plan_in,
+    index_in,
+    saved_ref,
+    gain_in,
+    down_ref,
+    up_ref,
+    head_in_ref,
+    head_gain_in,
+    targets_in,
+    levels_in,
+    grads_out,
+    down_out,
+    up_out,
+    head_out,
     plan_ref,
     index_ref,
-    saved_ref,
     gain_ref,
-    down_ref,
-    up_ref,
     head_ref,
     head_gain_ref,
     targets_ref,
     levels_ref,
-    grads_out,
-    down_out,
-    up_out,
-    head_out,
     saved,
     down,
     up,
@@ -140,6 +147,8 @@
     other_send,
     other_recv,
     ready,
+    small_sem,
+    out_sem,
 ):
     units, unit, width = wide.shape
     micro = saved.shape[0]
@@ -190,9 +199,20 @@
     saved_load = pltpu.make_async_copy(saved_ref, saved, load_sem.at[0])
     down_load = pltpu.make_async_copy(down_ref, down, load_sem.at[1])
     up_load = pltpu.make_async_copy(up_ref, up, load_sem.at[2])
-    saved_load.start()
-    down_load.start()
-    up_load.start()
+    small_loads = [
+        pltpu.make_async_copy(source, held, small_sem.at[number])
+        for number, (source, held) in enumerate(
+            (
+                (plan_in, plan_ref),
+                (gain_in, gain_ref),
+                (head_in_ref, head_ref),
+                (index_in, index_ref),
+                (head_gain_in, head_gain_ref),
+                (targets_in, targets_ref),
+                (levels_in, levels_ref),
+            )
+        )
+    ]
 
     barrier = pltpu.get_barrier_semaphore()
 
@@ -223,6 +243,15 @@
             def _():
                 greet((lax.div(block, replicas), lax.rem(block, replicas)))
 
+    saved_load.start()
+    for load in small_loads[:3]:
+        load.start()
+    down_load.start()
+    up_load.start()
+    for load in small_loads[3:]:
+        load.start()
+    for load in small_loads:
+        load.wait()
     saved_load.wait()
 
     def norm_slot(slot, unused):
@@ -640,14 +669,6 @@
     normed_far.wait_recv()
     normed_relay.start()
 
-    def relay_slot(slot, unused):
-        for number in range(per_slot):
-            far_copies(slot * per_slot + number)[2].wait_recv()
-        relay_copy(slot).start()
-        return unused
-
-    lax.fori_loop(0, micro, relay_slot, 0)
-
     def backs_arrived(slot, unused):
         slot_copies(slot)[1].wait_recv()
         for number in range(per_slot):
@@ -660,6 +681,15 @@
     normed_relay.wait_recv()
     multiply(0)
     ring_start(0)
+
+    def relay_slot(slot, unused):
+        for number in range(per_slot):
+            far_copies(slot * per_slot + number)[2].wait_recv()
+        relay_copy(slot).start()
+        return unused
+
+    lax.fori_loop(0, micro, relay_slot, 0)
+
     multiply(1)
     ring_start(1)
 
@@ -722,6 +752,18 @@
 
     mine = pl.ds(pl.multiple_of(core * half, half), half)
     theirs = pl.ds(pl.multiple_of((1 - core) * half, half), half)
+    results = (down_out, up_out)
+
+    def own_out(matrix):
+        return pltpu.make_async_copy(
+            halves.at[matrix, core], results[matrix].at[:, mine], out_sem.at[matrix]
+        )
+
+    def mate_out(matrix):
+        return pltpu.make_async_copy(
+            mates.at[matrix], results[matrix].at[:, theirs], out_sem.at[2 + matrix]
+        )
+
     halves[0, :, :, pl.ds(pl.multiple_of(side * quarter, quarter), quarter)] = (
         ring_total(1) / LOSS_SCALE
     ).reshape(2, share, quarter)
@@ -730,25 +772,30 @@
             ring_total(item) / LOSS_SCALE
         ).reshape(2, share, quarter)
     mate_copy(1).start()
-    up_out[:, mine] = halves[1, core]
+    own_out(1).start()
     across_copy.wait_recv()
     halves[0, :, :, pl.ds(pl.multiple_of((1 - side) * quarter, quarter), quarter)] = (
         across[...].astype(F32) / LOSS_SCALE
     ).reshape(2, share, quarter)
     mate_copy(0).start()
-    down_out[:, mine] = halves[0, core]
-
-    for matrix, result in ((1, up_out), (0, down_out)):
+    own_out(0).start()
+
+    for matrix in (1, 0):
         mate_copy(matrix).wait_recv()
-        result[:, theirs] = mates[matrix]
+        mate_out(matrix).start()
 
     @pl.when(jnp.logical_not(source_is_me))
     def _():
         share_copy(0)[1].wait_recv()
 
-    head_out[...] = head_mine[...]
+    head_write = pltpu.make_async_copy(head_mine, head_out, out_sem.at[4])
+    head_write.start()
 
     grads_copy.wait()
+    for matrix in range(2):
+        own_out(matrix).wait()
+        mate_out(matrix).wait()
+    head_write.wait()
     for copy in (
         normed_copy,
         normed_far,
@@ -850,7 +897,6 @@
     units_all = 2 * micro
     quarter = half // 2
     longest = rings // 2
-    whole = pl.BlockSpec(memory_space=pltpu.VMEM)
     anywhere = pl.BlockSpec(memory_space=pl.ANY)
     dma = pltpu.SemaphoreType.DMA
     grads, down_grad, up_grad, head_grad = pl.pallas_call(
@@ -861,20 +907,16 @@
             jax.ShapeDtypeStruct((share, units), F32),
             jax.ShapeDtypeStruct((final, cols), F32),
         ),
-        in_specs=[
-            pl.BlockSpec(memory_space=pltpu.SMEM),
-            whole,
-            anywhere,
-            whole,
-            anywhere,
-            anywhere,
-            whole,
-            whole,
-            whole,
-            whole,
-        ],
-        out_specs=(anywhere, whole, whole, whole),
+        in_specs=[anywhere] * 10,
+        out_specs=(anywhere,) * 4,
         scratch_shapes=[
+            pltpu.SMEM(plan.shape, jnp.int32),
+            pltpu.VMEM((1, level_index.shape[0]), jnp.int32),
+            pltpu.VMEM(norm_gain.shape, F32),
+            pltpu.VMEM(head_weight.shape, BF16),
+            pltpu.VMEM((1, width), F32),
+            pltpu.VMEM(targets.shape, F32),
+            pltpu.VMEM(levels.T.shape, F32),
             pltpu.VMEM((micro, tokens, width), BF16),
             pltpu.VMEM((width, units), BF16),
             pltpu.VMEM((width, units), BF16),
@@ -930,6 +972,8 @@
             dma(()),
             dma(()),
             pltpu.SemaphoreType.REGULAR,
+            dma((7,)),
+            dma((5,)),
         ],
         compiler_params=pltpu.CompilerParams(
             collective_id=0, has_side_effects=True, vmem_limit_bytes=56 * 1024 * 1024

time: 111 us -> 110 us (level)
    pallas_call x1, Pallas kernels: 107 us -> 106 us  [local(): pl.pallas_call(functools.partial(body, sections, replicas), out_shape=(ja...]
where the time goes in v8:
time: 110 us; the launch traced here: 108 us
  Pallas kernels  108 us (98%)
    pallas_call x1, Pallas kernels, local(): pl.pallas_call(functools.partial(body, sections, replicas), out_shape=(ja...  106 us

profile of v8, /device:TPU:1, one launch (start us, length us, event | category | flops | bytes accessed | tf_op | source)
XLA Modules:
  0.0 108.3 jit_solution(15344218699990072132)
XLA Ops:
  0.6 105.6 %shard_map.129 = (bf16[8,32,1024]{2,1,0:T(8,128)(2,1)}, f32[32,2048]{1,0:T(8,128)}, f32[32,2048]{1,0:T(8,128)}, f32[4,128]{1,0:T(4,128)}) custom-call(s32[4]{0:T(128)} %plan_in.1, s32[1,64]{1,0:T(1,128)} %bitcast.14, bf16[4,64,1024]{2,1,0:T(8,128)(2,1)} %bitcast.11, f32[1,1024]{1,0:T(1,128)} %gain_in.1, bf16[1024,2048]{1,0:T(8,128)(2,1)} %bitcast.9, ...), custom_call_target="tpu_custom_call" | custom-call | tf_op jit(solution)/shard_map/pallas_call | solution.py:902
  106.3 2.1 %shard_map.130 = (bf16[8,32,1024]{2,1,0:T(8,128)(2,1)}, f32[32,2048]{1,0:T(8,128)}, f32[32,2048]{1,0:T(8,128)}, f32[4,128]{1,0:T(4,128)}) custom-call(bf16[8,32,1024]{2,1,0:T(8,128)(2,1)} %get-tuple-element.12.refs_0_, f32[32,2048]{1,0:T(8,128)} %get-tuple-element.13.refs_1_, f32[32,2048]{1,0:T(8,128)} %get-tuple-element.14.refs_2_, ...), custom_call_target="tpu_custom_call" | custom-call | tf_op jit(solution)/shard_map/pallas_call | solution.py:993

commit v9 on v8

--- a/solution.py
+++ b/solution.py
@@ -594,11 +594,17 @@
 
     @pl.when(jnp.logical_not(streams))
     def _():
-        def send(number, unused):
-            send_far(number)
-            return unused
-
-        lax.fori_loop(0, units, send, 0)
+        def send_cots(number, unused):
+            far_copies(number)[2].start()
+            return unused
+
+        def send_backs(number, unused):
+            for copy in far_copies(number)[:2]:
+                copy.start()
+            return unused
+
+        lax.fori_loop(0, units, send_cots, 0)
+        lax.fori_loop(0, units, send_backs, 0)
 
     row_step = min(256, column_half)
     tokens_all = 4 * rows_all
@@ -666,9 +672,6 @@
             total = total + ring[item, way, last].astype(F32)
         return total
 
-    normed_far.wait_recv()
-    normed_relay.start()
-
     def backs_arrived(slot, unused):
         slot_copies(slot)[1].wait_recv()
         for number in range(per_slot):
@@ -676,74 +679,102 @@
                 copy.wait_recv()
         return unused
 
-    lax.fori_loop(0, micro, backs_arrived, 0)
-    normed_copy.wait_recv()
-    normed_relay.wait_recv()
-    multiply(0)
-    ring_start(0)
-
     def relay_slot(slot, unused):
         for number in range(per_slot):
             far_copies(slot * per_slot + number)[2].wait_recv()
         relay_copy(slot).start()
         return unused
 
-    lax.fori_loop(0, micro, relay_slot, 0)
-
-    multiply(1)
-    ring_start(1)
-
     def cots_arrived(slot, unused):
         slot_copies(slot)[0].wait_recv()
         relay_copy(slot).wait_recv()
         return unused
 
-    lax.fori_loop(0, micro, cots_arrived, 0)
-    for copy in (active_copy, active_far, active_cross):
-        copy.wait_recv()
-    multiply(2)
-    ring_start(2)
-    multiply(3)
-    ring_start(3)
-
-    @pl.when(is_last)
-    def _():
-        def add_term(offset, total):
-            term_wait(offset)
-            return total + head_terms[lax.rem(position + offset, positions)]
-
-        total = lax.fori_loop(1, positions, add_term, head_added[position]) / LOSS_SCALE
-        pl.semaphore_wait(ready, sections - jnp.where(me == replicas - 1, 1, 0))
-        for number in range(sections):
-            head_sums[number] = total[number * final : (number + 1) * final]
-        for number in range(sections):
-            block, copy = share_copy(number)
-            to_me = block == (sections - 1) * replicas + me
-
-            @pl.when(to_me)
-            def _():
-                head_mine[...] = head_sums[number]
-
-            @pl.when(jnp.logical_not(to_me))
-            def _():
-                copy.start()
-
     across_copy = remote(
         products.at[0, rows_of(level)], across, across_send.at[0], across_recv.at[0], opposite
     )
-    turns = (
-        ((0, 1), (1, 1), (2, 1), (0, 2), (3, 1), (1, 2), (0, 3), (2, 2), (3, 2), (1, 3), (2, 3), (3, 3))
-        if longest == 4
-        else tuple((item, hop) for hop in range(1, longest) for item in range(4))
-    )
-    for number, (item, hop) in enumerate(turns):
-        ring_turn(item, hop)
-        if number == len(turns) - 2:
-            products[0, rows_of(level)] = ring_total(0).astype(BF16)
-            across_copy.start()
-    if not turns:
+    def trade_across():
         products[0, rows_of(level)] = ring_total(0).astype(BF16)
         across_copy.start()
+
+    def down_arrived():
+        lax.fori_loop(0, micro, backs_arrived, 0)
+        normed_copy.wait_recv()
+        normed_relay.wait_recv()
+
+    def up_arrived():
+        lax.fori_loop(0, micro, cots_arrived, 0)
+        for copy in (active_copy, active_far, active_cross):
+            copy.wait_recv()
+
+    def make(item):
+        multiply(item)
+        ring_start(item)
+
+    normed_far.wait_recv()
+    normed_relay.start()
+
+    @pl.when(streams)
+    def _():
+        down_arrived()
+        make(0)
+        lax.fori_loop(0, micro, relay_slot, 0)
+        make(1)
+        up_arrived()
+        make(2)
+        make(3)
+        turns = (
+            ((0, 1), (1, 1), (2, 1), (0, 2), (3, 1), (1, 2), (0, 3), (2, 2), (3, 2), (1, 3), (2, 3), (3, 3))
+            if longest == 4
+            else tuple((item, hop) for hop in range(1, longest) for item in range(4))
+        )
+        for item, hop in turns[:-1]:
+            ring_turn(item, hop)
+        trade_across()
+        for item, hop in turns[-1:]:
+            ring_turn(item, hop)
+
+    @pl.when(jnp.logical_not(streams))
+    def _():
+        lax.fori_loop(0, micro, relay_slot, 0)
+        up_arrived()
+        make(2)
+        make(3)
+        @pl.when(is_last)
+        def _():
+            def add_term(offset, total):
+                term_wait(offset)
+                return total + head_terms[lax.rem(position + offset, positions)]
+
+            total = lax.fori_loop(1, positions, add_term, head_added[position]) / LOSS_SCALE
+            pl.semaphore_wait(ready, sections - jnp.where(me == replicas - 1, 1, 0))
+            for number in range(sections):
+                head_sums[number] = total[number * final : (number + 1) * final]
+            for number in range(sections):
+                block, copy = share_copy(number)
+                to_me = block == (sections - 1) * replicas + me
+
+                @pl.when(to_me)
+                def _():
+                    head_mine[...] = head_sums[number]
+
+                @pl.when(jnp.logical_not(to_me))
+                def _():
+                    copy.start()
+
+        for hop in range(1, longest - 1):
+            ring_turn(2, hop)
+            ring_turn(3, hop)
+        down_arrived()
+        make(0)
+        make(1)
+        for hop in range(1, longest):
+            ring_turn(0, hop)
+            ring_turn(1, hop)
+            if hop == 1:
+                ring_turn(2, longest - 1)
+                ring_turn(3, longest - 1)
+        trade_across()
 
     def mate_copy(matrix):
         return remote(

time: 110 us -> 109 us (level); the launches traced: 108 us -> 108 us
  no operation moved by 1% of the time
where the time goes in v9:
time: 109 us; the launch traced here: 108 us
  Pallas kernels  108 us (99%)
    pallas_call x1, Pallas kernels, local(): pl.pallas_call(functools.partial(body, sections, replicas), out_shape=(ja...  106 us

profile of v9, /device:TPU:1, one launch (start us, length us, event | category | flops | bytes accessed | tf_op | source)
XLA Modules:
  0.0 108.5 jit_solution(11656204472400515857)
XLA Ops:
  0.6 105.7 %shard_map.129 = (bf16[8,32,1024]{2,1,0:T(8,128)(2,1)}, f32[32,2048]{1,0:T(8,128)}, f32[32,2048]{1,0:T(8,128)}, f32[4,128]{1,0:T(4,128)}) custom-call(s32[4]{0:T(128)} %plan_in.1, s32[1,64]{1,0:T(1,128)} %bitcast.14, bf16[4,64,1024]{2,1,0:T(8,128)(2,1)} %bitcast.11, f32[1,1024]{1,0:T(1,128)} %gain_in.1, bf16[1024,2048]{1,0:T(8,128)(2,1)} %bitcast.9, ...), custom_call_target="tpu_custom_call" | custom-call | tf_op jit(solution)/shard_map/pallas_call | solution.py:933
  106.4 2.1 %shard_map.130 = (bf16[8,32,1024]{2,1,0:T(8,128)(2,1)}, f32[32,2048]{1,0:T(8,128)}, f32[32,2048]{1,0:T(8,128)}, f32[4,128]{1,0:T(4,128)}) custom-call(bf16[8,32,1024]{2,1,0:T(8,128)(2,1)} %get-tuple-element.12.refs_0_, f32[32,2048]{1,0:T(8,128)} %get-tuple-element.13.refs_1_, f32[32,2048]{1,0:T(8,128)} %get-tuple-element.14.refs_2_, ...), custom_call_target="tpu_custom_call" | custom-call | tf_op jit(solution)/shard_map/pallas_call | solution.py:1024

commit v10 on v9

--- a/solution.py
+++ b/solution.py
@@ -226,14 +226,14 @@
             greet(device)
 
     position = side * levels + level
+    farthest_first = sorted(
+        range(1, positions), key=lambda offset: -min(offset % levels, levels - offset % levels)
+    )
 
     @pl.when(is_last)
     def _():
-        def greet_peer(offset, unused):
+        for offset in farthest_first:
             greet((section, lax.rem(position + offset, positions) * 2 + core))
-            return unused
-
-        lax.fori_loop(1, positions, greet_peer, 0)
         greet(mate)
         greet(diagonal)
         for number in range(sections):
@@ -275,11 +275,6 @@
     )
     pl.semaphore_wait(barrier, heard)
 
-    @pl.when(jnp.logical_not(source_is_me))
-    def _():
-        pl.semaphore_signal(
-            ready, inc=1, device_id=(sections - 1, head_source), device_id_type=MESH
-        )
 
     def gather_copy(offset):
         peer = lax.rem(position + offset, positions)
@@ -312,12 +307,15 @@
 
     @pl.when(is_last)
     def _():
-        def send(offset, unused):
+        for offset in farthest_first:
             gather_copy(offset).start()
-            return unused
-
-        lax.fori_loop(1, positions, send, 0)
         full_head[position, core] = head_ref[...]
+
+    @pl.when(jnp.logical_not(source_is_me))
+    def _():
+        pl.semaphore_signal(
+            ready, inc=1, device_id=(sections - 1, head_source), device_id_type=MESH
+        )
 
     normed_copy = remote(normed.at[3], normed.at[0], pair_send.at[0], pair_recv.at[0], mate)
     normed_copy.start()
@@ -468,6 +466,9 @@
             if arriving:
                 cot_copy(first, piece).wait_recv()
             columns = slice(piece * column_half, (piece + 1) * column_half)
+            if not passing and piece == 1:
+                for number in range(count):
+                    far_copies(first + number)[2].start()
             part = matmul(cots[these, :, columns].reshape(rows, column_half), up[columns, :])
             back_active = part if back_active is None else back_active + part
         dot = jnp.zeros((rows, 1), F32)
@@ -484,6 +485,10 @@
                 back.astype(F32) * hiddens[part, these].reshape(rows, half), axis=-1, keepdims=True
             )
             back_parts.append(back)
+        if not passing:
+            for number in range(count):
+                for copy in far_copies(first + number)[:2]:
+                    copy.start()
         inverse = inverses[these].reshape(rows, 1)
         pull = inverse * inverse * dot * (1.0 / width)
         for piece in range(2):
@@ -505,7 +510,7 @@
         ours = pl.ds(pl.multiple_of(side * column_half, column_half), column_half)
         sided[3, these] = cots[these, :, ours]
 
-        if far:
+        if far and passing:
 
             @pl.when(streams)
             def _():

time: 109 us -> 107 us (0.982)
  Pallas kernels: 108 us -> 105 us
    pallas_call x1, Pallas kernels: 106 us -> 103 us  [local(): pl.pallas_call(functools.partial(body, sections, replicas), out_shape=(ja...]
where the time goes in v10:
time: 107 us; the launch traced here: 106 us
  Pallas kernels  105 us (98%)
    pallas_call x1, Pallas kernels, local(): pl.pallas_call(functools.partial(body, sections, replicas), out_shape=(ja...  103 us

profile of v10, /device:TPU:1, one launch (start us, length us, event | category | flops | bytes accessed | tf_op | source)
XLA Modules:
  0.0 106.1 jit_solution(8126584367977637613)
XLA Ops:
  0.6 103.3 %shard_map.129 = (bf16[8,32,1024]{2,1,0:T(8,128)(2,1)}, f32[32,2048]{1,0:T(8,128)}, f32[32,2048]{1,0:T(8,128)}, f32[4,128]{1,0:T(4,128)}) custom-call(s32[4]{0:T(128)} %plan_in.1, s32[1,64]{1,0:T(1,128)} %bitcast.14, bf16[4,64,1024]{2,1,0:T(8,128)(2,1)} %bitcast.11, f32[1,1024]{1,0:T(1,128)} %gain_in.1, bf16[1024,2048]{1,0:T(8,128)(2,1)} %bitcast.9, ...), custom_call_target="tpu_custom_call" | custom-call | tf_op jit(solution)/shard_map/pallas_call | solution.py:938
  104.0 2.1 %shard_map.130 = (bf16[8,32,1024]{2,1,0:T(8,128)(2,1)}, f32[32,2048]{1,0:T(8,128)}, f32[32,2048]{1,0:T(8,128)}, f32[4,128]{1,0:T(4,128)}) custom-call(bf16[8,32,1024]{2,1,0:T(8,128)(2,1)} %get-tuple-element.12.refs_0_, f32[32,2048]{1,0:T(8,128)} %get-tuple-element.13.refs_1_, f32[32,2048]{1,0:T(8,128)} %get-tuple-element.14.refs_2_, ...), custom_call_target="tpu_custom_call" | custom-call | tf_op jit(solution)/shard_map/pallas_call | solution.py:1029

commit v11 on v10

--- a/solution.py
+++ b/solution.py
@@ -781,9 +781,15 @@
                 ring_turn(3, longest - 1)
         trade_across()
 
-    def mate_copy(matrix):
+    def mate_copy(matrix, piece):
+        which = piece if matrix == 1 else lax.rem(side + piece, 2)
+        columns = pl.ds(pl.multiple_of(which * quarter, quarter), quarter)
         return remote(
-            halves.at[matrix, 1 - core], mates.at[matrix], mate_send.at[matrix], mate_recv.at[matrix], mate
+            halves.at[matrix, 1 - core, :, columns],
+            mates.at[matrix, :, columns],
+            mate_send.at[matrix, piece],
+            mate_recv.at[matrix, piece],
+            mate,
         )
 
     mine = pl.ds(pl.multiple_of(core * half, half), half)
@@ -803,21 +809,23 @@
     halves[0, :, :, pl.ds(pl.multiple_of(side * quarter, quarter), quarter)] = (
         ring_total(1) / LOSS_SCALE
     ).reshape(2, share, quarter)
+    mate_copy(0, 0).start()
     for item in (2, 3):
         halves[1, :, :, (item - 2) * quarter : (item - 1) * quarter] = (
             ring_total(item) / LOSS_SCALE
         ).reshape(2, share, quarter)
-    mate_copy(1).start()
+        mate_copy(1, item - 2).start()
     own_out(1).start()
     across_copy.wait_recv()
     halves[0, :, :, pl.ds(pl.multiple_of((1 - side) * quarter, quarter), quarter)] = (
         across[...].astype(F32) / LOSS_SCALE
     ).reshape(2, share, quarter)
-    mate_copy(0).start()
+    mate_copy(0, 1).start()
     own_out(0).start()
 
     for matrix in (1, 0):
-        mate_copy(matrix).wait_recv()
+        for piece in range(2):
+            mate_copy(matrix, piece).wait_recv()
         mate_out(matrix).start()
 
     @pl.when(jnp.logical_not(source_is_me))
@@ -868,7 +876,8 @@
             for hop in range(hops(item, way)):
                 ring_copy(item, way, hop).wait_send()
     for matrix in range(2):
-        mate_copy(matrix).wait_send()
+        for piece in range(2):
+            mate_copy(matrix, piece).wait_send()
 
     @pl.when(is_last)
     def _():
@@ -997,8 +1006,8 @@
             dma((4, 2, longest)),
             dma((1,)),
             dma((1,)),
-            dma((2,)),
-            dma((2,)),
+            dma((2, 2)),
+            dma((2, 2)),
             dma((replicas // 2,)),
             dma((replicas // 2 + 1,)),
             dma((replicas // 2,)),

time: 107 us -> 107 us (level)
  no operation moved by 1% of the time
where the time goes in v11:
time: 107 us; the launch traced here: 106 us
  Pallas kernels  105 us (98%)
    pallas_call x1, Pallas kernels, local(): pl.pallas_call(functools.partial(body, sections, replicas), out_shape=(ja...  103 us

profile of v11, /device:TPU:1, one launch (start us, length us, event | category | flops | bytes accessed | tf_op | source)
XLA Modules:
  0.0 106.1 jit_solution(16027185225277636799)
XLA Ops:
  0.6 103.4 %shard_map.129 = (bf16[8,32,1024]{2,1,0:T(8,128)(2,1)}, f32[32,2048]{1,0:T(8,128)}, f32[32,2048]{1,0:T(8,128)}, f32[4,128]{1,0:T(4,128)}) custom-call(s32[4]{0:T(128)} %plan_in.1, s32[1,64]{1,0:T(1,128)} %bitcast.14, bf16[4,64,1024]{2,1,0:T(8,128)(2,1)} %bitcast.11, f32[1,1024]{1,0:T(1,128)} %gain_in.1, bf16[1024,2048]{1,0:T(8,128)(2,1)} %bitcast.9, ...), custom_call_target="tpu_custom_call" | custom-call | tf_op jit(solution)/shard_map/pallas_call | solution.py:947
  104.0 2.1 %shard_map.130 = (bf16[8,32,1024]{2,1,0:T(8,128)(2,1)}, f32[32,2048]{1,0:T(8,128)}, f32[32,2048]{1,0:T(8,128)}, f32[4,128]{1,0:T(4,128)}) custom-call(bf16[8,32,1024]{2,1,0:T(8,128)(2,1)} %get-tuple-element.12.refs_0_, f32[32,2048]{1,0:T(8,128)} %get-tuple-element.13.refs_1_, f32[32,2048]{1,0:T(8,128)} %get-tuple-element.14.refs_2_, ...), custom_call_target="tpu_custom_call" | custom-call | tf_op jit(solution)/shard_map/pallas_call | solution.py:1038
